TPU v7x, 32 devices: a whole 2x2x4 slice. The times are simulated.
32 devices in a mesh: dp: 8 (over y, x, core), vocab: 4 (over z).
Axes of the slice: x: 2, y: 2, z: 4, core: 2. Of those that a mesh axis runs over, the one named last changes fastest.
Arguments:
- final_states: bfloat16 [4096, 5376], P(('dp', 'vocab')), may hold values from -12 to 12
- head_blocks: bfloat16 [4, 128, 5376], P('vocab'), may hold values from -0.17048273 to 0.17048273
- block_order: int32 [4], replicated, may hold values from 0 to 3, as said below
- row_tags: int32 [4096], P(('dp', 'vocab')), may hold values from 0 to 3, as said below
- target_word: int32 [4096], P(('dp', 'vocab')), may hold values from 0 to 127
- row_weight: bfloat16 [4096], P(('dp', 'vocab')), may hold values from 0.25 to 2
Outputs:
- row_loss: float32 [4096], P(('dp', 'vocab'))
- state_grad: bfloat16 [4096, 5376], P(('dp', 'vocab'))
- head_grad: float32 [4, 128, 5376], P('vocab', 'dp')
Inputs may be any that keep to these rules, and one draw needn't show every extreme that they name: `row_tags`: among the rows of one device at most 40 carry any one tag; one tag, the same on every device, is carried by exactly 40 rows of each device. Each block number appears once; the shortlist of tag l is block_order[l] to block_order[(l + 1) - 1].
All inputs are finite; a program needn't handle non-finite values.
Results may differ from a plain program's by a relative error of at most 0.0052.
Values may be sent and summed in bfloat16 or wider, within the bound.
A program may use at most 128 MiB of HBM per device.

v0:
```python
import jax
import jax.numpy as jnp
from jax import lax
from jax.sharding import PartitionSpec as P

BLOCK = 128
LANGS = 4


def shards(final_states, head_blocks, block_order, row_tags, target_word, row_weight):
    shard_count = lax.axis_size("vocab")
    rows_here = final_states.shape[0]
    short_len = shard_count // LANGS
    capacity = rows_here * 5 // 16
    block_ids = jnp.arange(shard_count, dtype=jnp.int32)
    placed = jnp.sum(
        block_ids[:, None] * (block_order[:, None] == block_ids[None, :]).astype(jnp.int32), axis=0
    )
    owner_tag = placed // short_len
    owner_slot = placed % short_len
    tag_ids = jnp.arange(LANGS, dtype=jnp.int32)
    tag_onehot = (row_tags[:, None] == tag_ids[None, :]).astype(jnp.int32)
    row_rank = jnp.sum((jnp.cumsum(tag_onehot, axis=0) - 1) * tag_onehot, axis=1)
    routed = owner_tag[:, None] == row_tags[None, :]
    slot_ids = jnp.arange(capacity, dtype=jnp.int32)
    chosen = routed[:, None, :] & (row_rank[None, None, :] == slot_ids[None, :, None])
    chosen_int = chosen.astype(jnp.int32)
    slot_used = jnp.sum(chosen_int, axis=2) > 0
    row_ids = jnp.arange(rows_here, dtype=jnp.int32)
    slot_row = jnp.sum(chosen_int * row_ids[None, None, :], axis=2)
    sent_rows = jnp.where(
        slot_used[:, :, None], jnp.take(final_states, slot_row, axis=0), jnp.zeros((), jnp.bfloat16)
    )
    local_word = jnp.where(
        target_word[None, :] // BLOCK == owner_slot[:, None], target_word[None, :] % BLOCK, -1
    )
    slot_word = jnp.sum(chosen_int * (local_word[:, None, :] + 1), axis=2) - 1
    slot_label = jnp.where(slot_used, slot_row, -1)
    slot_weight = jnp.sum(
        jnp.where(chosen, row_weight.astype(jnp.float32)[None, None, :], 0.0), axis=2
    ).astype(jnp.bfloat16)
    got_rows, got_label, got_word, got_weight = (
        lax.all_to_all(sent_rows, "vocab", split_axis=0, concat_axis=0, tiled=True),
        lax.all_to_all(slot_label, "vocab", split_axis=0, concat_axis=0, tiled=True),
        lax.all_to_all(slot_word, "vocab", split_axis=0, concat_axis=0, tiled=True),
        lax.all_to_all(slot_weight, "vocab", split_axis=0, concat_axis=0, tiled=True),
    )
    own_block = head_blocks[0]
    logits = jnp.einsum("scd,wd->scw", got_rows, own_block, preferred_element_type=jnp.float32)
    word_ids = jnp.arange(BLOCK, dtype=jnp.int32)
    target_hit = word_ids[None, None, :] == got_word[:, :, None]
    slot_peak = jnp.max(logits, axis=2)
    slot_total = jnp.sum(jnp.exp(logits - slot_peak[:, :, None]), axis=2)
    slot_picked = jnp.sum(jnp.where(target_hit, logits, 0.0), axis=2)
    back_peak, back_total, back_picked = (
        lax.all_to_all(slot_peak, "vocab", split_axis=0, concat_axis=0, tiled=True),
        lax.all_to_all(slot_total, "vocab", split_axis=0, concat_axis=0, tiled=True),
        lax.all_to_all(slot_picked, "vocab", split_axis=0, concat_axis=0, tiled=True),
    )
    row_peak = jnp.take(back_peak, row_rank, axis=1)
    row_total = jnp.take(back_total, row_rank, axis=1)
    row_picked = jnp.take(back_picked, row_rank, axis=1)
    peak_max = jnp.max(jnp.where(routed, row_peak, -1e30), axis=0)
    summed = jnp.sum(
        jnp.where(routed, row_total * jnp.exp(row_peak - peak_max[None, :]), 0.0), axis=0
    )
    log_total = peak_max + jnp.log(summed)
    row_loss = log_total - jnp.sum(jnp.where(routed, row_picked, 0.0), axis=0)
    slot_lse = jnp.where(slot_used, jnp.take(log_total, slot_row), 0.0)
    got_lse = lax.all_to_all(slot_lse, "vocab", split_axis=0, concat_axis=0, tiled=True)
    slot_probs = jnp.exp(logits - got_lse[:, :, None])
    slot_grads = (
        got_weight.astype(jnp.float32)[:, :, None] * (slot_probs - target_hit.astype(jnp.float32))
    ).astype(jnp.bfloat16)
    part_grads = jnp.einsum(
        "scw,wd->scd", slot_grads, own_block, preferred_element_type=jnp.float32
    ).astype(jnp.bfloat16)
    back_grads = lax.all_to_all(part_grads, "vocab", split_axis=0, concat_axis=0, tiled=True)
    state_grad = jnp.einsum(
        "sct,scd->td", chosen.astype(jnp.bfloat16), back_grads, preferred_element_type=jnp.float32
    ).astype(jnp.bfloat16)
    head_term = jnp.einsum("scw,scd->wd", slot_grads, got_rows, preferred_element_type=jnp.float32)
    head_share = lax.psum_scatter(head_term, "dp", scatter_dimension=0, tiled=True)
    return (row_loss, state_grad, head_share[None])


def solution(mesh):
    return jax.shard_map(
        shards,
        mesh=mesh,
        in_specs=(
            P(("dp", "vocab"), None),
            P("vocab", None, None),
            P(),
            P(("dp", "vocab")),
            P(("dp", "vocab")),
            P(("dp", "vocab")),
        ),
        out_specs=(P(("dp", "vocab")), P(("dp", "vocab"), None), P("vocab", "dp", None)),
        check_vma=False,
    )
```

profile of v0, /device:TPU:0, one launch (start us, length us, event | category | flops | bytes accessed | tf_op | source)
XLA Modules:
  0.0 170.8 jit_solution(14118096110840504848)
XLA Ops:
  7.2 0.0 copy-start
  7.2 0.8 and_select_fusion.4
  8.0 0.7 fusion.17
  8.6 0.7 select_reduce_fusion.2
  9.4 0.7 fusion.14
  10.1 0.7 broadcast_compare_fusion
  10.8 0.1 copy.30
  10.9 0.2 reduce_window_sum.11
  11.1 0.8 select_reduce_fusion.1
  12.0 0.3 fusion.7
  12.3 0.1 reshape.256
  12.4 4.8 %gather_fusion = bf16[160,5376]{1,0:T(8,128)(2,1)S(1)} fusion(bf16[128,5376]{1,0:T(8,128)(2,1)} %param.8, s32[1024]{0:T(1024)S(1)} %pad_clamp_fusion.1), kind=kCustom, calls=%fused_computation.3 | custom fusion | bytes 3441280 | tf_op jit(solution)/shard_map/jit(_take)/gather | solution.py:32
  17.2 1.5 select_select_fusion
  18.7 6.3 %all-to-all-start = ((bf16[4,40,5376]{2,1,0:T(8,128)(2,1)}), bf16[4,40,5376]{2,1,0:T(8,128)(2,1)S(1)}, u32[]{:S(2)}, u32[]{:S(2)}) async-start(bf16[4,40,5376]{2,1,0:T(8,128)(2,1)} %select_select_fusion), calls=%async_computation | async-start | bytes 3440640 | tf_op jit(solution)/shard_map/all_to_all | solution.py:43
  25.0 0.0 copy-start.2
  25.0 0.6 broadcast_add_fusion
  25.6 39.5 %all-to-all-done = bf16[4,40,5376]{2,1,0:T(8,128)(2,1)S(1)} async-done(((bf16[4,40,5376]{2,1,0:T(8,128)(2,1)}), bf16[4,40,5376]{2,1,0:T(8,128)(2,1)S(1)}, u32[]{:S(2)}, u32[]{:S(2)}) %all-to-all-start) | async-done | bytes 1720352 | tf_op jit(solution)/shard_map/all_to_all | solution.py:43
  65.1 3.2 %all-to-all-start.3 = ((s32[4,1,40]{2,1,0:T(1,128)}), s32[4,1,40]{2,1,0:T(1,128)S(1)}, u32[]{:S(2)}, u32[]{:S(2)}) async-start(s32[4,1,40]{2,1,0:T(1,128)} %bitcast.12), calls=%async_computation.3 | async-start | bytes 4096 | tf_op jit(solution)/shard_map/all_to_all | solution.py:45
  68.4 0.0 copy-done
  68.4 0.0 copy-start.1
  68.4 1.3 fusion.19
  69.7 4.1 %all-to-all-done.3 = s32[4,1,40]{2,1,0:T(1,128)S(1)} async-done(((s32[4,1,40]{2,1,0:T(1,128)}), s32[4,1,40]{2,1,0:T(1,128)S(1)}, u32[]{:S(2)}, u32[]{:S(2)}) %all-to-all-start.3) | async-done | bytes 672 | tf_op jit(solution)/shard_map/all_to_all | solution.py:45
  73.8 1.5 select_reduce_fusion
  75.3 3.2 %all-to-all-start.2 = ((f32[4,1,40]{2,1,0:T(1,128)}), f32[4,1,40]{2,1,0:T(1,128)S(1)}, u32[]{:S(2)}, u32[]{:S(2)}) async-start(f32[4,1,40]{2,1,0:T(1,128)} %bitcast.9), calls=%async_computation.2 | async-start | bytes 4096 | tf_op jit(solution)/shard_map/all_to_all | solution.py:57
  78.6 0.0 copy-done.2
  78.6 5.3 %all-to-all-done.2 = f32[4,1,40]{2,1,0:T(1,128)S(1)} async-done(((f32[4,1,40]{2,1,0:T(1,128)}), f32[4,1,40]{2,1,0:T(1,128)S(1)}, u32[]{:S(2)}, u32[]{:S(2)}) %all-to-all-start.2) | async-done | bytes 672 | tf_op jit(solution)/shard_map/all_to_all | solution.py:57
  83.9 3.2 %all-to-all-start.1 = ((f32[4,1,40]{2,1,0:T(1,128)}), f32[4,1,40]{2,1,0:T(1,128)S(1)}, u32[]{:S(2)}, u32[]{:S(2)}) async-start(f32[4,1,40]{2,1,0:T(1,128)} %bitcast.5), calls=%async_computation.1 | async-start | bytes 4096 | tf_op jit(solution)/shard_map/all_to_all | solution.py:56
  87.1 0.1 fusion.8
  87.2 5.3 %all-to-all-done.1 = f32[4,1,40]{2,1,0:T(1,128)S(1)} async-done(((f32[4,1,40]{2,1,0:T(1,128)}), f32[4,1,40]{2,1,0:T(1,128)S(1)}, u32[]{:S(2)}, u32[]{:S(2)}) %all-to-all-start.1) | async-done | bytes 672 | tf_op jit(solution)/shard_map/all_to_all | solution.py:56
  92.6 3.2 %all-to-all-start.4 = ((f32[4,1,40]{2,1,0:T(1,128)}), f32[4,1,40]{2,1,0:T(1,128)S(1)}, u32[]{:S(2)}, u32[]{:S(2)}) async-start(f32[4,1,40]{2,1,0:T(1,128)} %bitcast.15), calls=%async_computation.4 | async-start | bytes 4096 | tf_op jit(solution)/shard_map/all_to_all | solution.py:58
  95.8 0.6 copy.37
  96.4 0.1 copy.32
  96.5 0.6 gather_fusion.2
  97.1 0.1 copy.34
  97.2 0.6 gather_fusion.3
  97.9 3.4 %all-to-all-done.4 = f32[4,1,40]{2,1,0:T(1,128)S(1)} async-done(((f32[4,1,40]{2,1,0:T(1,128)}), f32[4,1,40]{2,1,0:T(1,128)S(1)}, u32[]{:S(2)}, u32[]{:S(2)}) %all-to-all-start.4) | async-done | bytes 672 | tf_op jit(solution)/shard_map/all_to_all | solution.py:58
  101.2 3.2 %all-to-all-start.5 = ((bf16[4,1,40]{2,1,0:T(2,128)(2,1)}), bf16[4,1,40]{2,1,0:T(2,128)(2,1)S(1)}, u32[]{:S(2)}, u32[]{:S(2)}) async-start(bf16[4,1,40]{2,1,0:T(2,128)(2,1)} %copy.37), calls=%async_computation.5 | async-start | bytes 4096 | tf_op jit(solution)/shard_map/all_to_all | solution.py:46
  104.5 0.1 copy.36
  104.6 0.6 gather_fusion.4
  105.2 0.0 copy-done.1
  105.2 0.2 fusion.12
  105.4 0.2 fusion.9
  105.6 0.5 fusion.18
  106.2 1.5 gather_fusion.1
  107.7 0.1 gather.15
  107.8 0.6 copy_select_fusion
  108.4 1.5 all-to-all-done.5
  109.8 3.6 %all-to-all-start.6 = ((f32[4,1,40]{2,1,0:T(1,128)}), f32[4,1,40]{2,1,0:T(1,128)S(1)}, u32[]{:S(2)}, u32[]{:S(2)}) async-start(f32[4,1,40]{2,1,0:T(1,128)} %copy_select_fusion), calls=%async_computation.6 | async-start | bytes 4096 | tf_op jit(solution)/shard_map/all_to_all | solution.py:70
  113.4 0.0 reduce-scatter.2.cloned.1.call-start
  113.5 5.5 %all-to-all-done.6 = f32[4,1,40]{2,1,0:T(1,128)S(1)} async-done(((f32[4,1,40]{2,1,0:T(1,128)}), f32[4,1,40]{2,1,0:T(1,128)S(1)}, u32[]{:S(2)}, u32[]{:S(2)}) %all-to-all-start.6) | async-done | bytes 672 | tf_op jit(solution)/shard_map/all_to_all | solution.py:70
  118.9 2.2 %convolution_bitcast_fusion = f32[128,5376]{1,0:T(8,128)} fusion(bf16[4,40,5376]{2,1,0:T(8,128)(2,1)S(1)} %all-to-all-done, f32[4,40,128]{2,1,0:T(8,128)S(1)} %get-tuple-element.14, f32[4,40]{1,0:T(4,128)S(1)} %bitcast.71, f32[4,40]{1,0:T(4,128)S(1)} %bitcast.73, s32[4,40]{1,0:T(4,128)S(1)} %bitcast.68), kind=kOutput, calls=%fused_computation.5 | convolution fusion | flops 220323840 | bytes 4556672 | tf_op jit(solution)/shard_map/scw,scd->wd/dot_general | solution.py:82
  121.1 0.0 reduce-scatter.2.cloned.1.call-update
  121.2 0.7 convolution_convert_fusion
  121.9 35.9 %all_to_all.64 = bf16[4,40,5376]{2,1,0:T(8,128)(2,1)S(1)} all-to-all(bf16[4,40,5376]{2,1,0:T(8,128)(2,1)S(1)} %convolution_convert_fusion), channel_id=1, replica_groups=mesh['dp'=8,'vocab'=4] {'vocab'}, dimensions={0} | all-to-all | bytes 3440640 | tf_op jit(solution)/shard_map/all_to_all | solution.py:78
  157.7 1.6 fusion
  159.4 4.6 %reduce-scatter.2.cloned.1.call-done = f32[16,5376]{1,0:T(8,128)} async-done(((f32[128,5376]{1,0:T(8,128)}), f32[16,5376]{1,0:T(8,128)}) %reduce-scatter.2.cloned.1.call-update) | async-done | bytes 344080 | tf_op jit(solution)/shard_map/reduce_scatter | solution.py:83
  (10 shorter events, 0.1 us)
Async XLA Ops:
  7.2 61.2 %copy-start = (bf16[1,128,5376]{2,1,0:T(8,128)(2,1)S(1)}, bf16[1,128,5376]{2,1,0:T(8,128)(2,1)}, u32[]{:S(2)}) copy-start(bf16[1,128,5376]{2,1,0:T(8,128)(2,1)} %param.9) | copy-start | bytes 4128772
  18.7 46.4 %all-to-all-start = ((bf16[4,40,5376]{2,1,0:T(8,128)(2,1)}), bf16[4,40,5376]{2,1,0:T(8,128)(2,1)S(1)}, u32[]{:S(2)}, u32[]{:S(2)}) async-start(bf16[4,40,5376]{2,1,0:T(8,128)(2,1)} %select_select_fusion), calls=%async_computation | async-start | bytes 3440640 | tf_op jit(solution)/shard_map/all_to_all | solution.py:43
  25.0 53.5 %copy-start.2 = (bf16[128]{0:T(256)(128)(2,1)S(1)}, bf16[128]{0:T(256)(128)(2,1)}, u32[]{:S(2)}) copy-start(bf16[128]{0:T(256)(128)(2,1)} %param.13) | copy-start | bytes 772
  65.1 8.7 %all-to-all-start.3 = ((s32[4,1,40]{2,1,0:T(1,128)}), s32[4,1,40]{2,1,0:T(1,128)S(1)}, u32[]{:S(2)}, u32[]{:S(2)}) async-start(s32[4,1,40]{2,1,0:T(1,128)} %bitcast.12), calls=%async_computation.3 | async-start | bytes 4096 | tf_op jit(solution)/shard_map/all_to_all | solution.py:45
  68.4 36.9 %copy-start.1 = (s32[128]{0:T(128)S(1)}, s32[128]{0:T(128)}, u32[]{:S(2)}) copy-start(s32[128]{0:T(128)} %param.11) | copy-start | bytes 1540
  75.3 8.6 %all-to-all-start.2 = ((f32[4,1,40]{2,1,0:T(1,128)}), f32[4,1,40]{2,1,0:T(1,128)S(1)}, u32[]{:S(2)}, u32[]{:S(2)}) async-start(f32[4,1,40]{2,1,0:T(1,128)} %bitcast.9), calls=%async_computation.2 | async-start | bytes 4096 | tf_op jit(solution)/shard_map/all_to_all | solution.py:57
  83.9 8.7 %all-to-all-start.1 = ((f32[4,1,40]{2,1,0:T(1,128)}), f32[4,1,40]{2,1,0:T(1,128)S(1)}, u32[]{:S(2)}, u32[]{:S(2)}) async-start(f32[4,1,40]{2,1,0:T(1,128)} %bitcast.5), calls=%async_computation.1 | async-start | bytes 4096 | tf_op jit(solution)/shard_map/all_to_all | solution.py:56
  92.6 8.7 %all-to-all-start.4 = ((f32[4,1,40]{2,1,0:T(1,128)}), f32[4,1,40]{2,1,0:T(1,128)S(1)}, u32[]{:S(2)}, u32[]{:S(2)}) async-start(f32[4,1,40]{2,1,0:T(1,128)} %bitcast.15), calls=%async_computation.4 | async-start | bytes 4096 | tf_op jit(solution)/shard_map/all_to_all | solution.py:58
  101.2 8.6 %all-to-all-start.5 = ((bf16[4,1,40]{2,1,0:T(2,128)(2,1)}), bf16[4,1,40]{2,1,0:T(2,128)(2,1)S(1)}, u32[]{:S(2)}, u32[]{:S(2)}) async-start(bf16[4,1,40]{2,1,0:T(2,128)(2,1)} %copy.37), calls=%async_computation.5 | async-start | bytes 4096 | tf_op jit(solution)/shard_map/all_to_all | solution.py:46
  109.8 9.1 %all-to-all-start.6 = ((f32[4,1,40]{2,1,0:T(1,128)}), f32[4,1,40]{2,1,0:T(1,128)S(1)}, u32[]{:S(2)}, u32[]{:S(2)}) async-start(f32[4,1,40]{2,1,0:T(1,128)} %copy_select_fusion), calls=%async_computation.6 | async-start | bytes 4096 | tf_op jit(solution)/shard_map/all_to_all | solution.py:70
  113.4 50.6 %reduce-scatter.2.cloned.1.call-start = ((), (), s32[]{:S(2)}) async-start(), calls=%async_computation.9 | async-start | bytes 3096576 | tf_op jit(solution)/shard_map/reduce_scatter | solution.py:83
Sparse Core Ops, SparseCore 0:
  121.3 42.6 reduce-scatter.1
where the time goes:
time: 171 us
  waiting for transfers between devices  69.2 us (40%)
  blocking collectives  35.9 us (21%)
  starting transfers between devices  26.1 us (15%)
  between operations  14.2 us (8%)
  other arithmetic  10.2 us (6%)
  local copies, waits for them, and re-layouts  9.38 us (5%)
  matrix products  5.87 us (3%)
    all_to_all x1, waiting for transfers between devices, shards(): lax.all_to_all(sent_rows, 'vocab', split_axis=0, concat_axis=0, tiled=True)  39.5 us
    all_to_all x1, blocking collectives, shards(): lax.all_to_all(part_grads, 'vocab', split_axis=0, concat_axis=0, tiled=True)  35.9 us
    all_to_all x1, starting transfers between devices, shards(): lax.all_to_all(sent_rows, 'vocab', split_axis=0, concat_axis=0, tiled=True)  6.32 us
    all_to_all x1, waiting for transfers between devices, shards(): lax.all_to_all(slot_lse, 'vocab', split_axis=0, concat_axis=0, tiled=True)  5.46 us
    all_to_all x1, waiting for transfers between devices, shards(): lax.all_to_all(slot_peak, 'vocab', split_axis=0, concat_axis=0, tiled=True)  5.33 us
    all_to_all x1, waiting for transfers between devices, shards(): lax.all_to_all(slot_total, 'vocab', split_axis=0, concat_axis=0, tiled=True)  5.33 us
    gather x1, local copies, waits for them, and re-layouts, shards(): jnp.take(final_states, slot_row, axis=0)  4.78 us
    reduce_scatter x1, waiting for transfers between devices, shards(): lax.psum_scatter(head_term, 'dp', scatter_dimension=0, tiled=True)  4.61 us
  transfers between devices with their start and end apart: 8, of which 8 were waited for; matrix products, arithmetic and copies ran while one was open for 6% of the time, Pallas kernels for 0%

commit v1 on v0

--- a/solution.py
+++ b/solution.py
@@ -1,10 +1,376 @@
 import jax
 import jax.numpy as jnp
 from jax import lax
+from jax.experimental import pallas as pl
+from jax.experimental.pallas import tpu as pltpu
 from jax.sharding import PartitionSpec as P
 
 BLOCK = 128
 LANGS = 4
+MESH = pl.DeviceIdType.MESH
+F32 = jnp.float32
+BF16 = jnp.bfloat16
+PARTS = 8
+
+
+def dot(a, b, dims):
+    return lax.dot_general(a, b, ((dims[:1], dims[1:]), ((), ())), preferred_element_type=F32)
+
+
+def iota(shape, dim):
+    return lax.broadcasted_iota(jnp.int32, shape, dim)
+
+
+def routed_kernel(
+    order, tags, words, weights, states, block,
+    loss_out, state_out, head_out,
+    head_here, send_rows, got_rows, send_meta, got_meta, send_back, got_back, send_loss, got_loss,
+    pick_lo, pick_hi, grads_lo, grads_hi, term, pair_send, pair_got, plane_send, plane_got, line_got,
+    row_s, row_r, meta_s, meta_r, back_s, back_r, loss_s, loss_r, pair_s, pair_r, plane_s, plane_r,
+    line_s, line_r, up_s, down_s, head_r, twin_s, twin_r,
+):
+    rows, width = states.shape
+    half = width // 2
+    cap = rows * 5 // 16
+    tall = 2 * cap
+    words_each = BLOCK // (2 * LANGS)
+    step = max(s for s in range(128, 513, 128) if half % s == 0)
+    steps = half // step
+
+    dp, z = lax.axis_index("dp"), lax.axis_index("vocab")
+    last = lax.axis_size("vocab") - 1
+    core = lax.rem(dp, 2)
+    x = lax.rem(lax.div(dp, 2), 2)
+    y = lax.div(dp, 4)
+    chips = [(y if r < 2 else 1 - y) * 2 + (x if r % 2 == 0 else 1 - x) for r in range(4)]
+    own = chips[0]
+    plane = [(c * 2 + core, z) for c in chips]
+    twin = (own * 2 + 1 - core, z)
+    line = [(dp, lax.rem(z + d, LANGS)) for d in range(LANGS)]
+
+    barrier = pltpu.get_barrier_semaphore()
+    friends = plane[1:] + line[1:] + [twin]
+    for friend in friends:
+        pl.semaphore_signal(barrier, inc=1, device_id=friend, device_id_type=MESH)
+
+    def remote(src, dst, send, recv, to):
+        return pltpu.make_async_remote_copy(
+            src_ref=src, dst_ref=dst, send_sem=send, recv_sem=recv, device_id=to, device_id_type=MESH
+        )
+
+    sub = iota((16, rows), 0)
+    wanted = jnp.full((16, rows), -1, jnp.int32)
+    for r in range(4):
+        tag = jnp.int32(0)
+        for l in range(LANGS):
+            tag = tag + jnp.where(order[l] == chips[r], l, 0)
+        wanted = jnp.where(sub == r, tag, wanted)
+    mask = wanted == jnp.broadcast_to(tags[...], (16, rows))
+    before = jnp.where(iota((rows, rows), 0) < iota((rows, rows), 1), 1.0, 0.0).astype(BF16)
+    rank = dot(jnp.where(mask, 1.0, 0.0).astype(BF16), before, (1, 0))
+    rank = jnp.where(mask, rank, -1000.0).astype(jnp.int32)
+    meta = jnp.where(
+        sub == 0,
+        jnp.broadcast_to(words[...].astype(F32), (16, rows)),
+        jnp.where(sub == 1, jnp.broadcast_to(weights[...].astype(F32), (16, rows)), 0.0),
+    ).astype(BF16)
+
+    def slots(r, height):
+        return iota((height, rows), 0) == jnp.broadcast_to(rank[r : r + 1], (height, rows))
+
+    spans = [pl.ds(r * tall, tall) for r in range(4)]
+    for r in range(4):
+        slot = iota((tall, rows), 0)
+        key = jnp.broadcast_to(rank[r : r + 1], (tall, rows))
+        pick_lo[spans[r], :] = jnp.where(slot == key, 1.0, 0.0).astype(BF16)
+        pick_hi[spans[r], :] = jnp.where(slot == key + cap, 1.0, 0.0).astype(BF16)
+        here = dot(meta, jnp.where(slots(r, rows), 1.0, 0.0).astype(BF16), (1, 1)).astype(BF16)
+        if r:
+            send_meta[r] = here
+        else:
+            got_meta[0] = here
+
+    pl.semaphore_wait(barrier, len(friends))
+
+    def part(ref, i):
+        row = pl.multiple_of((BLOCK // 2) * core + 16 * lax.div(i, 2), 16)
+        col = pl.multiple_of(half * lax.rem(i, 2), 128)
+        return ref.at[pl.ds(row, 16), pl.ds(col, half)]
+
+    def up(src, i):
+        return remote(part(src, i), part(head_here, i), up_s.at[i], head_r.at[i], (dp, lax.rem(z + 1, LANGS)))
+
+    def down(src, i):
+        return remote(
+            part(src, i), part(head_here, i), down_s.at[i], head_r.at[i], (dp, lax.rem(z + LANGS - 1, LANGS))
+        )
+
+    def to_twin(i):
+        return remote(part(head_here, i), part(head_here, i), twin_s.at[i], twin_r.at[i], twin)
+
+    goes_up = (z >= own) & (z < last)
+    goes_down = (z <= own) & (z > 0)
+    is_source = z == own
+
+    @pl.when(is_source)
+    def _():
+        @pl.loop(0, PARTS)
+        def _(i):
+            @pl.when(z < last)
+            def _():
+                up(block, i).start()
+
+            @pl.when(z > 0)
+            def _():
+                down(block, i).start()
+
+    row_copies = {}
+    for r in (3, 1, 2, 0):
+        target = send_rows if r else got_rows
+
+        @pl.loop(0, steps)
+        def _(j, r=r, target=target):
+            lo = pl.ds(pl.multiple_of(j * step, 128), step)
+            hi = pl.ds(pl.multiple_of(half + j * step, 128), step)
+            target[spans[r], lo] = (
+                dot(pick_lo[spans[r], :], states[:, lo], (1, 0)) + dot(pick_hi[spans[r], :], states[:, hi], (1, 0))
+            ).astype(BF16)
+
+        if r:
+            row_copies[r] = (
+                remote(send_meta.at[r], got_meta.at[r], meta_s.at[r - 1], meta_r.at[r - 1], plane[r]),
+                remote(
+                    send_rows.at[spans[r], :], got_rows.at[spans[r], :], row_s.at[r - 1], row_r.at[r - 1], plane[r]
+                ),
+            )
+            for copy in row_copies[r]:
+                copy.start()
+
+    @pl.when(is_source)
+    def _():
+        head_here[...] = block[...]
+
+    @pl.when(jnp.logical_not(is_source))
+    def _():
+        @pl.loop(0, PARTS)
+        def _(i):
+            up(head_here, i).wait_recv()
+
+            @pl.when(goes_up)
+            def _():
+                up(head_here, i).start()
+
+            @pl.when(goes_down)
+            def _():
+                down(head_here, i).start()
+
+            to_twin(i).start()
+
+        @pl.loop(0, PARTS)
+        def _(i):
+            to_twin(i).wait_recv()
+
+    for r in (1, 2, 3):
+        for copy in row_copies[r]:
+            copy.wait_recv()
+
+    first = dot(got_rows[...], head_here[:, :half], (1, 1)).reshape(4, tall, BLOCK)
+    second = dot(got_rows[...], head_here[:, half:], (1, 1)).reshape(4, tall, BLOCK)
+    eye = jnp.where(iota((cap, BLOCK), 0) == iota((cap, BLOCK), 1), 1.0, 0.0)
+    lane = iota((cap, BLOCK), 1)
+    empty = jnp.zeros((cap, BLOCK), F32)
+    for r in range(4):
+        logits = first[r, :cap] + second[r, cap:]
+        facts = dot(eye.astype(BF16), got_meta[r], (1, 1))
+        hit = lane == facts[:, 0:1].astype(jnp.int32)
+        peak = jnp.max(logits, axis=1, keepdims=True)
+        total = peak + jnp.log(jnp.sum(jnp.exp(logits - peak), axis=1, keepdims=True))
+        picked = jnp.sum(jnp.where(hit, logits, 0.0), axis=1, keepdims=True)
+        losses = jnp.sum(jnp.where(eye > 0.0, total - picked, 0.0), axis=0, keepdims=True)
+        losses = jnp.broadcast_to(losses, (8, BLOCK))
+        if r:
+            send_loss[r] = losses
+        else:
+            got_loss[0] = losses
+        grads = facts[:, 1:2] * (jnp.exp(logits - total) - jnp.where(hit, 1.0, 0.0))
+        grads_lo[spans[r], :] = jnp.concatenate([grads, empty], axis=0).astype(BF16)
+        grads_hi[spans[r], :] = jnp.concatenate([empty, grads], axis=0).astype(BF16)
+
+    @pl.loop(0, steps)
+    def _(j):
+        lo = pl.ds(pl.multiple_of(j * step, 128), step)
+        hi = pl.ds(pl.multiple_of(half + j * step, 128), step)
+        term[:, lo] = dot(grads_lo[...], got_rows[:, lo], (0, 0))
+        term[:, hi] = dot(grads_hi[...], got_rows[:, lo], (0, 0))
+
+    def words_of(r, which):
+        return pl.ds(pl.multiple_of(chips[r] * 2 * words_each + which * words_each, 16), words_each)
+
+    for r in range(4):
+        pair_send[r] = term[words_of(r, 1 - core), :].astype(BF16)
+    pair = remote(pair_send, pair_got, pair_s, pair_r, twin)
+    pair.start()
+
+    back_copies = {}
+
+    def give_back(r):
+        target = send_back if r else got_back
+
+        @pl.loop(0, steps)
+        def _(j):
+            lo = pl.ds(pl.multiple_of(j * step, 128), step)
+            hi = pl.ds(pl.multiple_of(half + j * step, 128), step)
+            target[spans[r], lo] = (
+                dot(grads_lo[spans[r], :], head_here[:, lo], (1, 0))
+                + dot(grads_hi[spans[r], :], head_here[:, hi], (1, 0))
+            ).astype(BF16)
+
+        if r:
+            back_copies[r] = (
+                remote(send_loss.at[r], got_loss.at[r], loss_s.at[r - 1], loss_r.at[r - 1], plane[r]),
+                remote(
+                    send_back.at[spans[r], :], got_back.at[spans[r], :], back_s.at[r - 1], back_r.at[r - 1], plane[r]
+                ),
+            )
+            for copy in back_copies[r]:
+                copy.start()
+
+    give_back(3)
+    pair.wait_recv()
+    plane_copies = {}
+    for r in (3, 1, 2, 0):
+        whole = (term[words_of(r, core), :] + pair_got[r].astype(F32)).astype(BF16)
+        if r:
+            plane_send[r] = whole
+            plane_copies[r] = remote(
+                plane_send.at[r], plane_got.at[r], plane_s.at[r - 1], plane_r.at[r - 1], plane[r]
+            )
+            plane_copies[r].start()
+        else:
+            plane_got[0] = whole
+    for r in (1, 2, 0):
+        give_back(r)
+    for r in (1, 2, 3):
+        plane_copies[r].wait_recv()
+
+    def place_of(chip):
+        return 2 * lax.rem(lax.div(chip, 2) + y, 2) + lax.rem(lax.rem(chip, 2) + x, 2)
+
+    line_copies = []
+    for d in range(1, LANGS):
+        copy = remote(
+            plane_got.at[place_of(line[d][1])], line_got.at[d - 1], line_s.at[d - 1], line_r.at[d - 1], line[d]
+        )
+        copy.start()
+        line_copies.append(copy)
+
+    for r in (1, 2, 3):
+        for copy in back_copies[r]:
+            copy.wait_recv()
+
+    @pl.loop(0, steps)
+    def _(j):
+        lo = pl.ds(pl.multiple_of(j * step, 128), step)
+        hi = pl.ds(pl.multiple_of(half + j * step, 128), step)
+        state_out[:, lo] = dot(pick_lo[...], got_back[:, lo], (0, 0)).astype(BF16)
+        state_out[:, hi] = dot(pick_hi[...], got_back[:, lo], (0, 0)).astype(BF16)
+
+    square = iota((rows, rows), 0) == iota((rows, rows), 1)
+    loss = jnp.zeros((1, rows), F32)
+    for r in range(4):
+        column = jnp.sum(
+            jnp.where(square, jnp.broadcast_to(got_loss[r, 0:1, :], (rows, rows)), 0.0), axis=1, keepdims=True
+        )
+        loss = loss + jnp.sum(jnp.where(slots(r, rows), column, 0.0), axis=0, keepdims=True)
+    loss_out[...] = loss
+
+    for copy in line_copies:
+        copy.wait_recv()
+    head_out[0] = (
+        plane_got[place_of(z)].astype(F32)
+        + line_got[0].astype(F32)
+        + line_got[1].astype(F32)
+        + line_got[2].astype(F32)
+    )
+
+    for r in (1, 2, 3):
+        for copy in (*row_copies[r], *back_copies[r], plane_copies[r]):
+            copy.wait_send()
+    pair.wait_send()
+    for copy in line_copies:
+        copy.wait_send()
+
+    @pl.loop(0, PARTS)
+    def _(i):
+        @pl.when(goes_up)
+        def _():
+            up(head_here, i).wait_send()
+
+        @pl.when(goes_down)
+        def _():
+            down(head_here, i).wait_send()
+
+        @pl.when(jnp.logical_not(is_source))
+        def _():
+            to_twin(i).wait_send()
+
+
+def routed(final_states, head_blocks, block_order, row_tags, target_word, row_weight):
+    rows, width = final_states.shape
+    cap = rows * 5 // 16
+    half = width // 2
+    stack = LANGS * 2 * cap
+    share = BLOCK // (2 * LANGS)
+    vmem = pl.BlockSpec(memory_space=pltpu.VMEM)
+    dma = pltpu.SemaphoreType.DMA
+    loss, state_grad, head_grad = pl.pallas_call(
+        routed_kernel,
+        out_shape=(
+            jax.ShapeDtypeStruct((1, rows), F32),
+            jax.ShapeDtypeStruct((rows, width), BF16),
+            jax.ShapeDtypeStruct((1, share, width), F32),
+        ),
+        in_specs=[pl.BlockSpec(memory_space=pltpu.SMEM)] + [vmem] * 5,
+        out_specs=(vmem, vmem, vmem),
+        scratch_shapes=[
+            pltpu.VMEM((BLOCK, width), BF16),
+            pltpu.VMEM((stack, half), BF16),
+            pltpu.VMEM((stack, half), BF16),
+            pltpu.VMEM((LANGS, 16, rows), BF16),
+            pltpu.VMEM((LANGS, 16, rows), BF16),
+            pltpu.VMEM((stack, half), BF16),
+            pltpu.VMEM((stack, half), BF16),
+            pltpu.VMEM((LANGS, 8, BLOCK), F32),
+            pltpu.VMEM((LANGS, 8, BLOCK), F32),
+            pltpu.VMEM((stack, rows), BF16),
+            pltpu.VMEM((stack, rows), BF16),
+            pltpu.VMEM((stack, BLOCK), BF16),
+            pltpu.VMEM((stack, BLOCK), BF16),
+            pltpu.VMEM((BLOCK, width), F32),
+            pltpu.VMEM((LANGS, share, width), BF16),
+            pltpu.VMEM((LANGS, share, width), BF16),
+            pltpu.VMEM((LANGS, share, width), BF16),
+            pltpu.VMEM((LANGS, share, width), BF16),
+            pltpu.VMEM((LANGS - 1, share, width), BF16),
+            dma((3,)), dma((3,)), dma((3,)), dma((3,)),
+            dma((3,)), dma((3,)), dma((3,)), dma((3,)),
+            dma, dma, dma((3,)), dma((3,)),
+            dma((3,)), dma((3,)),
+            dma((PARTS,)), dma((PARTS,)), dma((PARTS,)), dma((PARTS,)), dma((PARTS,)),
+        ],
+        compiler_params=pltpu.CompilerParams(
+            collective_id=0, has_side_effects=True, vmem_limit_bytes=40 * 1024 * 1024
+        ),
+        name="routed",
+    )(
+        block_order,
+        row_tags.reshape(1, rows),
+        target_word.reshape(1, rows),
+        row_weight.reshape(1, rows),
+        final_states,
+        head_blocks.reshape(BLOCK, width),
+    )
+    return loss.reshape(rows), state_grad, head_grad
 
 
 def shards(final_states, head_blocks, block_order, row_tags, target_word, row_weight):
@@ -85,8 +451,9 @@
 
 
 def solution(mesh):
+    one_each = mesh.shape["vocab"] == LANGS and mesh.shape["dp"] == 2 * LANGS
     return jax.shard_map(
-        shards,
+        routed if one_each else shards,
         mesh=mesh,
         in_specs=(
             P(("dp", "vocab"), None),

time: 171 us -> 75.6 us (0.44)
  waiting for transfers between devices: 69.2 us -> 0 us
  Pallas kernels: 0 us -> 66.4 us
  blocking collectives: 35.9 us -> 0 us
  starting transfers between devices: 26.1 us -> 0 us
  between operations: 14.2 us -> 0.65 us
  other arithmetic: 10.2 us -> 0 us
  matrix products: 5.87 us -> 0 us
  local copies, waits for them, and re-layouts: 9.38 us -> 7.61 us
    pallas_call x0 -> x1, Pallas kernels: none -> 66.4 us  [routed(): pl.pallas_call(routed_kernel, out_shape=(jax.ShapeDtypeStruct((1, rows),...]
    all_to_all x7 -> x0, waiting for transfers between devices: 64.6 us -> none  [the longest x1 39.5 us: shards(): lax.all_to_all(sent_rows, 'vocab', split_axis=0, concat_axis=0, tiled=True)]
    all_to_all x1 -> x0, blocking collectives: 35.9 us -> none  [shards(): lax.all_to_all(part_grads, 'vocab', split_axis=0, concat_axis=0, tiled=True)]
    all_to_all x7 -> x0, starting transfers between devices: 26.1 us -> none  [the longest x1 6.32 us: shards(): lax.all_to_all(sent_rows, 'vocab', split_axis=0, concat_axis=0, tiled=True)]
    gather x6 -> x0, local copies, waits for them, and re-layouts: 8.34 us -> none  [the longest x1 4.78 us: shards(): jnp.take(final_states, slot_row, axis=0)]
    unnamed x6 -> x15, local copies, waits for them, and re-layouts: 0.02 us -> 7.61 us
    dot_general x4 -> x0, matrix products: 5.87 us -> none  [the longest x1 2.22 us: shards(): jnp.einsum('scw,scd->wd', slot_grads, got_rows, preferred_element_type=jn...]
    reduce_scatter x1 -> x0, waiting for transfers between devices: 4.61 us -> none  [shards(): lax.psum_scatter(head_term, 'dp', scatter_dimension=0, tiled=True)]
  transfers between devices with their start and end apart: 8 -> 0, of which waited for: 8 -> 0; matrix products, arithmetic and copies ran while one was open for 6% -> 0% of each run, Pallas kernels for 0% -> 0%
where the time goes in v1:
time: 75.6 us; the launch traced here: 74.7 us
  Pallas kernels  66.4 us (88%)
  local copies, waits for them, and re-layouts  7.61 us (10%)
    pallas_call x1, Pallas kernels, routed(): pl.pallas_call(routed_kernel, out_shape=(jax.ShapeDtypeStruct((1, rows),...  66.4 us
    unnamed x15, local copies, waits for them, and re-layouts  7.61 us

profile of v1, /device:TPU:0, one launch (start us, length us, event | category | flops | bytes accessed | tf_op | source)
XLA Modules:
  0.0 74.7 jit_solution(14594397586690745862)
XLA Ops:
  0.6 0.0 copy-start
  0.6 1.3 %copy-done = bf16[128,5376]{1,0:T(8,128)(2,1)S(1)} copy-done((bf16[128,5376]{1,0:T(8,128)(2,1)S(1)}, bf16[128,5376]{1,0:T(8,128)(2,1)}, u32[]{:S(2)}) %copy-start) | copy-done | bytes 1376280
  2.0 0.0 copy-start.1
  2.0 1.3 %copy-done.1 = bf16[1,128,5376]{2,1,0:T(8,128)(2,1)S(1)} copy-done((bf16[1,128,5376]{2,1,0:T(8,128)(2,1)S(1)}, bf16[1,128,5376]{2,1,0:T(8,128)(2,1)}, u32[]{:S(2)}) %copy-start.1) | copy-done | bytes 1376280
  3.3 0.0 copy-start.2
  3.3 0.7 copy-done.2
  4.0 0.0 copy-start.3
  4.0 0.7 copy-done.3
  4.6 0.0 copy-start.4
  4.6 0.7 copy-done.4
  5.3 0.0 copy-start.5
  5.3 0.7 copy-done.5
  5.9 66.4 %routed.1 = (f32[1,128]{1,0:T(1,128)S(1)}, bf16[128,5376]{1,0:T(8,128)(2,1)S(1)}, f32[1,16,5376]{2,1,0:T(8,128)S(1)}) custom-call(s32[4]{0:T(128)S(1)} %copy-done.2, s32[1,128]{1,0:T(1,128)S(1)} %bitcast.6, s32[1,128]{1,0:T(1,128)S(1)} %bitcast.7, bf16[1,128]{1,0:T(2,128)(2,1)S(1)} %bitcast.8, bf16[128,5376]{1,0:T(8,128)(2,1)S(1)} %copy-done, ...), custom_call_target="tpu_custom_call" | custom-call | tf_op jit(solution)/shard_map/routed/pallas_call | solution.py:326
  72.4 0.5 copy.12
  72.9 1.1 %copy.13 = bf16[128,5376]{1,0:T(8,128)(2,1)} copy(bf16[128,5376]{1,0:T(8,128)(2,1)S(1)} %get-tuple-element.13) | data formatting | bytes 2752512
  74.0 0.7 copy.14
Async XLA Ops:
  0.6 1.3 %copy-start = (bf16[128,5376]{1,0:T(8,128)(2,1)S(1)}, bf16[128,5376]{1,0:T(8,128)(2,1)}, u32[]{:S(2)}) copy-start(bf16[128,5376]{1,0:T(8,128)(2,1)} %states.1) | copy-start | bytes 4128772
  2.0 1.3 %copy-start.1 = (bf16[1,128,5376]{2,1,0:T(8,128)(2,1)S(1)}, bf16[1,128,5376]{2,1,0:T(8,128)(2,1)}, u32[]{:S(2)}) copy-start(bf16[1,128,5376]{2,1,0:T(8,128)(2,1)} %param.7) | copy-start | bytes 4128772
  3.3 0.7 copy-start.2
  4.0 0.7 copy-start.3
  4.6 0.7 copy-start.4
  5.3 0.7 copy-start.5

commit v2 on v0

--- a/solution.py
+++ b/solution.py
@@ -1,10 +1,403 @@
 import jax
 import jax.numpy as jnp
 from jax import lax
+from jax.experimental import pallas as pl
+from jax.experimental.pallas import tpu as pltpu
 from jax.sharding import PartitionSpec as P
 
 BLOCK = 128
 LANGS = 4
+MESH = pl.DeviceIdType.MESH
+F32 = jnp.float32
+BF16 = jnp.bfloat16
+BATCHES = 2
+
+
+def dot(a, b, dims):
+    return lax.dot_general(a, b, ((dims[:1], dims[1:]), ((), ())), preferred_element_type=F32)
+
+
+def iota(shape, dim):
+    return lax.broadcasted_iota(jnp.int32, shape, dim)
+
+
+def slice_width(width):
+    return 128 * (-(-width // (128 * LANGS)))
+
+
+def sliced_kernel(
+    order_in, tags_in, words_in, weights_in, states, block,
+    loss_out, back_out, head_out,
+    order, tags, words, weights, cols, head, owner, part_send, part_got, grads, spread,
+    back_send, term, pair_send, pair_got, line_send, line_got, plane_send,
+    small_s, own_s, tag_s, tag_r, head_s, head_r, twin_s, twin_r, row_s, row_r,
+    part_s, part_r, grad_s, grad_r, back_s, back_r, pair_s, pair_r, line_s, line_r, plane_s, plane_r,
+):
+    rows, width = states.shape
+    wide = slice_width(width)
+    over = LANGS * wide - width
+    batch = rows // BATCHES
+    half = BLOCK // 2
+    share = BLOCK // (2 * LANGS)
+
+    dp, z = lax.axis_index("dp"), lax.axis_index("vocab")
+    core = lax.rem(dp, 2)
+    x = lax.rem(lax.div(dp, 2), 2)
+    y = lax.div(dp, 4)
+    chips = [(y if r < 2 else 1 - y) * 2 + (x if r % 2 == 0 else 1 - x) for r in range(4)]
+    own = chips[0]
+    plane = [(c * 2 + core, z) for c in chips]
+    twin = (own * 2 + 1 - core, z)
+    planes = [lax.rem(z + d, LANGS) for d in range(LANGS)]
+    sources = [lax.rem(z + LANGS - d, LANGS) for d in range(LANGS)]
+
+    def remote(src, dst, send, recv, to):
+        return pltpu.make_async_remote_copy(
+            src_ref=src, dst_ref=dst, send_sem=send, recv_sem=recv, device_id=to, device_id_type=MESH
+        )
+
+    def features(chip):
+        return pl.ds(pl.multiple_of(jnp.minimum(chip * wide, width - wide), 128), wide)
+
+    def span(b, r):
+        return pl.ds((b * 4 + r) * batch, batch)
+
+    def words_at(plane_id, first, count):
+        return pl.ds(pl.multiple_of(plane_id * BLOCK + first, 16), count)
+
+    barrier = pltpu.get_barrier_semaphore()
+    friends = plane[1:] + [(dp, planes[d]) for d in range(1, LANGS)] + [twin]
+    for friend in friends:
+        pl.semaphore_signal(barrier, inc=1, device_id=friend, device_id_type=MESH)
+
+    small = [
+        pltpu.make_async_copy(order_in, order, small_s.at[0]),
+        pltpu.make_async_copy(tags_in, tags.at[0], small_s.at[1]),
+        pltpu.make_async_copy(words_in, words, small_s.at[2]),
+        pltpu.make_async_copy(weights_in, weights, small_s.at[3]),
+    ]
+    mine = [pltpu.make_async_copy(block.at[:, features(own)], head.at[words_at(z, 0, BLOCK), :], own_s.at[BATCHES])]
+    for b in range(BATCHES):
+        here = states.at[pl.ds(b * batch, batch), features(own)]
+        mine.append(pltpu.make_async_copy(here, cols.at[span(b, 0), :], own_s.at[b]))
+    for copy in small + mine:
+        copy.start()
+
+    pl.semaphore_wait(barrier, len(friends))
+
+    head_copies = []
+    for d in (2, 1, 3):
+        copy = remote(
+            block.at[pl.ds(pl.multiple_of(half * core, 16), half), features(own)],
+            head.at[words_at(z, half * core, half), :],
+            head_s.at[d - 1], head_r.at[d - 1], (dp, planes[d]),
+        )
+        copy.start()
+        head_copies.append(copy)
+    tag_copies = []
+    for r in (3, 1, 2):
+        copy = remote(tags_in, tags.at[r], tag_s.at[r - 1], tag_r.at[r - 1], plane[r])
+        copy.start()
+        tag_copies.append(copy)
+    row_copies = [[], []]
+    for b in range(BATCHES):
+        for r in (3, 1, 2):
+            n = b * 3 + r - 1
+            copy = remote(
+                states.at[pl.ds(b * batch, batch), features(chips[r])],
+                cols.at[span(b, r), :],
+                row_s.at[n], row_r.at[n], plane[r],
+            )
+            copy.start()
+            row_copies[b].append(copy)
+
+    for copy in small:
+        copy.wait()
+    square = iota((rows, rows), 0) == iota((rows, rows), 1)
+    lane = iota((rows, BLOCK), 1)
+
+    def column(values):
+        wide_values = jnp.broadcast_to(values, (rows, rows))
+        return jnp.sum(jnp.where(square, wide_values, 0.0), axis=1, keepdims=True)
+
+    for copy in tag_copies:
+        copy.wait_recv()
+    for r in range(4):
+        tag = column(tags[r].astype(F32))
+        number = jnp.zeros((rows, 1), F32)
+        for l in range(LANGS):
+            number = jnp.where(tag == l, order[l].astype(F32), number)
+        number = jnp.broadcast_to(number, (rows, BLOCK))
+        for b in range(BATCHES):
+            owner[span(b, r), :] = number[b * batch : (b + 1) * batch]
+    target = column(words[...].astype(F32)).astype(jnp.int32)
+    weight = column(weights[...].astype(F32))
+
+    twin_copies = []
+    for d in (1, 2, 3):
+        remote(
+            head.at[words_at(sources[d], half * core, half), :],
+            head.at[words_at(sources[d], half * core, half), :],
+            head_s.at[d - 1], head_r.at[d - 1], (dp, planes[d]),
+        ).wait_recv()
+        copy = remote(
+            head.at[words_at(sources[d], half * core, half), :],
+            head.at[words_at(sources[d], half * core, half), :],
+            twin_s.at[d - 1], twin_r.at[d - 1], twin,
+        )
+        copy.start()
+        twin_copies.append(copy)
+    for copy in twin_copies:
+        copy.wait_recv()
+    mine[0].wait()
+
+    part_copies = [[] for _ in range(BATCHES)]
+    grad_copies = [[] for _ in range(BATCHES)]
+    back_copies = []
+    losses = []
+
+    def whole(b):
+        return pl.ds(b * 4 * batch, 4 * batch)
+
+    def partial_logits(b):
+        mine[1 + b].wait()
+        for copy in row_copies[b]:
+            copy.wait_recv()
+
+        if over:
+            @pl.when(own == LANGS - 1)
+            def _():
+                cols[whole(b), :over] = jnp.zeros((4 * batch, over), BF16)
+
+        every = dot(cols[whole(b), :], head[...], (1, 1))
+        number = owner[whole(b), :]
+        kept = jnp.zeros((4 * batch, BLOCK), F32)
+        for n in range(LANGS):
+            kept = jnp.where(number == n, every[:, n * BLOCK : (n + 1) * BLOCK], kept)
+        part_got[span(b, 0), :] = kept[:batch]
+        for r in (3, 1, 2):
+            n = b * 3 + r - 1
+            part_send[span(b, r), :] = kept[r * batch : (r + 1) * batch]
+            copy = remote(part_send.at[span(b, r), :], part_got.at[span(b, r), :], part_s.at[n], part_r.at[n], plane[r])
+            copy.start()
+            part_copies[b].append(copy)
+
+    def softmax_grads(b):
+        for copy in part_copies[b]:
+            copy.wait_recv()
+        pick = slice(b * batch, (b + 1) * batch)
+        logits = (part_got[span(b, 0), :] + part_got[span(b, 1), :]) + (
+            part_got[span(b, 2), :] + part_got[span(b, 3), :]
+        )
+        hit = lane[pick] == target[pick]
+        peak = jnp.max(logits, axis=1, keepdims=True)
+        total = peak + jnp.log(jnp.sum(jnp.exp(logits - peak), axis=1, keepdims=True))
+        losses.append(total - jnp.sum(jnp.where(hit, logits, 0.0), axis=1, keepdims=True))
+        grads[span(b, 0), :] = (weight[pick] * (jnp.exp(logits - total) - jnp.where(hit, 1.0, 0.0))).astype(BF16)
+        for r in (3, 1, 2):
+            n = b * 3 + r - 1
+            copy = remote(grads.at[span(b, 0), :], grads.at[span(b, r), :], grad_s.at[n], grad_r.at[n], plane[r])
+            copy.start()
+            grad_copies[b].append(copy)
+
+    def spread_grads(b):
+        for copy in grad_copies[b]:
+            copy.wait_recv()
+        number = owner[whole(b), :]
+        values = grads[whole(b), :].astype(F32)
+        for n in range(LANGS):
+            spread[whole(b), pl.ds(n * BLOCK, BLOCK)] = jnp.where(number == n, values, 0.0).astype(BF16)
+
+    def give_back(b):
+        back_send[whole(b), :] = dot(spread[whole(b), :], head[...], (1, 0)).astype(BF16)
+        for r in (3, 1, 2):
+            n = b * 3 + r - 1
+            copy = remote(
+                back_send.at[span(b, r), :],
+                back_out.at[own, pl.ds(b * batch, batch), :],
+                back_s.at[n], back_r.at[n], plane[r],
+            )
+            copy.start()
+            back_copies.append(copy)
+        copy = pltpu.make_async_copy(
+            back_send.at[span(b, 0), :], back_out.at[own, pl.ds(b * batch, batch), :], own_s.at[BATCHES + 1 + b]
+        )
+        copy.start()
+        mine.append(copy)
+
+    for b in range(BATCHES):
+        partial_logits(b)
+    for b in range(BATCHES):
+        softmax_grads(b)
+    for b in range(BATCHES):
+        spread_grads(b)
+        if b == 0:
+            give_back(0)
+
+    def mine_of(e, which):
+        return pl.ds(pl.multiple_of(2 * share * e + share * which, 16), share)
+
+    pair_copies = {}
+    for d in (2, 1, 3, 0):
+        picked = spread[:, pl.ds(pl.multiple_of(planes[d] * BLOCK, 128), BLOCK)]
+        term[d] = dot(picked, cols[...], (0, 0))
+        for e in range(LANGS):
+            pair_send[d, pl.ds(e * share, share), :] = term[d, mine_of(e, 1 - core), :].astype(BF16)
+        pair_copies[d] = remote(pair_send.at[d], pair_got.at[d], pair_s.at[d], pair_r.at[d], twin)
+        pair_copies[d].start()
+
+    line_copies = []
+
+    def both(d, e):
+        return term[d, mine_of(e, core), :] + pair_got[d, pl.ds(e * share, share), :].astype(F32)
+
+    for d in (2, 1, 3):
+        pair_copies[d].wait_recv()
+        for e in range(LANGS):
+            line_send[d - 1, pl.ds(e * share, share), :] = both(d, e).astype(BF16)
+        copy = remote(
+            line_send.at[d - 1], line_got.at[d - 1], line_s.at[d - 1], line_r.at[d - 1], (dp, planes[d])
+        )
+        copy.start()
+        line_copies.append(copy)
+
+    for b in range(1, BATCHES):
+        give_back(b)
+
+    loss = jnp.concatenate(losses, axis=0)
+    loss_out[...] = jnp.sum(jnp.where(square, loss, 0.0), axis=0, keepdims=True)
+
+    pair_copies[0].wait_recv()
+    for copy in line_copies:
+        copy.wait_recv()
+    for e in range(LANGS):
+        part = pl.ds(e * share, share)
+        plane_send[e] = (
+            (both(0, e) + line_got[0, part, :].astype(F32))
+            + (line_got[1, part, :].astype(F32) + line_got[2, part, :].astype(F32))
+        ).astype(BF16)
+    plane_copies = []
+    for r in (3, 1, 2):
+        copy = remote(
+            plane_send.at[chips[r]], head_out.at[own], plane_s.at[r - 1], plane_r.at[r - 1], plane[r]
+        )
+        copy.start()
+        plane_copies.append(copy)
+    copy = pltpu.make_async_copy(plane_send.at[own], head_out.at[own], own_s.at[2 * BATCHES + 1])
+    copy.start()
+    mine.append(copy)
+
+    for copy in back_copies + plane_copies:
+        copy.wait_recv()
+    for copy in mine[1 + BATCHES :]:
+        copy.wait()
+    everything = (
+        head_copies + tag_copies + twin_copies + back_copies + line_copies + plane_copies
+        + [c for group in row_copies + part_copies + grad_copies for c in group]
+        + [pair_copies[d] for d in range(LANGS)]
+    )
+    for copy in everything:
+        copy.wait_send()
+
+
+def joined_kernel(loss_in, back_in, head_in, loss_out, state_out, head_out, head_got, head_done, sems):
+    wide = back_in.shape[2]
+    over = LANGS * wide - state_out.shape[1]
+    fetch = pltpu.make_async_copy(head_in, head_got, sems.at[0])
+    fetch.start()
+    copies = [pltpu.make_async_copy(loss_in, loss_out, sems.at[1])]
+    for e in range(LANGS):
+        skip = over if e == LANGS - 1 else 0
+        here = pl.ds(e * wide, wide - skip)
+        copies.append(
+            pltpu.make_async_copy(back_in.at[e, :, pl.ds(skip, wide - skip)], state_out.at[:, here], sems.at[2 + e])
+        )
+    for copy in copies:
+        copy.start()
+    fetch.wait()
+    for e in range(LANGS):
+        skip = over if e == LANGS - 1 else 0
+        head_done[0, :, pl.ds(e * wide, wide - skip)] = head_got[e, :, pl.ds(skip, wide - skip)].astype(F32)
+    store = pltpu.make_async_copy(head_done, head_out, sems.at[2 + LANGS])
+    store.start()
+    for copy in copies:
+        copy.wait()
+    store.wait()
+
+
+def sliced(final_states, head_blocks, block_order, row_tags, target_word, row_weight):
+    rows, width = final_states.shape
+    wide = slice_width(width)
+    over = LANGS * wide - width
+    share = BLOCK // (2 * LANGS)
+    half = BLOCK // 2
+    group = LANGS * rows
+    hbm = pl.BlockSpec(memory_space=pl.ANY)
+    vmem = pl.BlockSpec(memory_space=pltpu.VMEM)
+    dma = pltpu.SemaphoreType.DMA
+    three, batches = dma((3,)), dma((3 * BATCHES,))
+    loss, back, head = pl.pallas_call(
+        sliced_kernel,
+        out_shape=(
+            jax.ShapeDtypeStruct((1, rows), F32),
+            jax.ShapeDtypeStruct((LANGS, rows, wide), BF16),
+            jax.ShapeDtypeStruct((LANGS, share, wide), BF16),
+        ),
+        in_specs=[hbm] * 6,
+        out_specs=(vmem, hbm, hbm),
+        scratch_shapes=[
+            pltpu.SMEM((LANGS,), jnp.int32),
+            pltpu.VMEM((LANGS, 1, rows), jnp.int32),
+            pltpu.VMEM((1, rows), jnp.int32),
+            pltpu.VMEM((1, rows), BF16),
+            pltpu.VMEM((group, wide), BF16),
+            pltpu.VMEM((LANGS * BLOCK, wide), BF16),
+            pltpu.VMEM((group, BLOCK), F32),
+            pltpu.VMEM((group, BLOCK), F32),
+            pltpu.VMEM((group, BLOCK), F32),
+            pltpu.VMEM((group, BLOCK), BF16),
+            pltpu.VMEM((group, LANGS * BLOCK), BF16),
+            pltpu.VMEM((group, wide), BF16),
+            pltpu.VMEM((LANGS, BLOCK, wide), F32),
+            pltpu.VMEM((LANGS, half, wide), BF16),
+            pltpu.VMEM((LANGS, half, wide), BF16),
+            pltpu.VMEM((LANGS - 1, half, wide), BF16),
+            pltpu.VMEM((LANGS - 1, half, wide), BF16),
+            pltpu.VMEM((LANGS, share, wide), BF16),
+            dma((4,)), dma((2 * BATCHES + 2,)), three, three, three, three, three, three, batches, batches,
+            batches, batches, batches, batches, batches, batches, dma((LANGS,)), dma((LANGS,)),
+            three, three, three, three,
+        ],
+        compiler_params=pltpu.CompilerParams(
+            collective_id=0, has_side_effects=True, vmem_limit_bytes=60 * 1024 * 1024
+        ),
+        name="sliced",
+    )(
+        block_order,
+        row_tags.reshape(1, rows),
+        target_word.reshape(1, rows),
+        row_weight.reshape(1, rows),
+        final_states,
+        head_blocks.reshape(BLOCK, width),
+    )
+    loss, state_grad, head_grad = pl.pallas_call(
+        joined_kernel,
+        out_shape=(
+            jax.ShapeDtypeStruct((1, rows), F32),
+            jax.ShapeDtypeStruct((rows, width), BF16),
+            jax.ShapeDtypeStruct((1, share, width), F32),
+        ),
+        in_specs=[hbm] * 3,
+        out_specs=[hbm] * 3,
+        scratch_shapes=[
+            pltpu.VMEM((LANGS, share, wide), BF16),
+            pltpu.VMEM((1, share, width), F32),
+            dma((LANGS + 3,)),
+        ],
+        compiler_params=pltpu.CompilerParams(vmem_limit_bytes=60 * 1024 * 1024),
+        name="joined",
+    )(loss, back, head)
+    return loss.reshape(rows), state_grad, head_grad
 
 
 def shards(final_states, head_blocks, block_order, row_tags, target_word, row_weight):
@@ -85,8 +478,9 @@
 
 
 def solution(mesh):
+    one_each = mesh.shape["vocab"] == LANGS and mesh.shape["dp"] == 2 * LANGS
     return jax.shard_map(
-        shards,
+        sliced if one_each else shards,
         mesh=mesh,
         in_specs=(
             P(("dp", "vocab"), None),

time: 171 us -> 97.9 us (0.57)
  Pallas kernels: 0 us -> 96.3 us
  waiting for transfers between devices: 69.2 us -> 0 us
  blocking collectives: 35.9 us -> 0 us
  starting transfers between devices: 26.1 us -> 0 us
  between operations: 14.2 us -> 0.64 us
  other arithmetic: 10.2 us -> 0 us
  local copies, waits for them, and re-layouts: 9.38 us -> 0 us
  matrix products: 5.87 us -> 0 us
    pallas_call x0 -> x2, Pallas kernels: none -> 96.3 us  [the longest x1 53.4 us: sliced(): pl.pallas_call(sliced_kernel, out_shape=(jax.ShapeDtypeStruct((1, rows),...]
    all_to_all x7 -> x0, waiting for transfers between devices: 64.6 us -> none  [the longest x1 39.5 us: shards(): lax.all_to_all(sent_rows, 'vocab', split_axis=0, concat_axis=0, tiled=True)]
    all_to_all x1 -> x0, blocking collectives: 35.9 us -> none  [shards(): lax.all_to_all(part_grads, 'vocab', split_axis=0, concat_axis=0, tiled=True)]
    all_to_all x7 -> x0, starting transfers between devices: 26.1 us -> none  [the longest x1 6.32 us: shards(): lax.all_to_all(sent_rows, 'vocab', split_axis=0, concat_axis=0, tiled=True)]
    gather x6 -> x0, local copies, waits for them, and re-layouts: 8.34 us -> none  [the longest x1 4.78 us: shards(): jnp.take(final_states, slot_row, axis=0)]
    dot_general x4 -> x0, matrix products: 5.87 us -> none  [the longest x1 2.22 us: shards(): jnp.einsum('scw,scd->wd', slot_grads, got_rows, preferred_element_type=jn...]
    reduce_scatter x1 -> x0, waiting for transfers between devices: 4.61 us -> none  [shards(): lax.psum_scatter(head_term, 'dp', scatter_dimension=0, tiled=True)]
    reduce_sum x6 -> x0, other arithmetic: 3.66 us -> none  [the longest x1 1.49 us: shards(): slot_picked = jnp.sum(jnp.where(target_hit, logits, 0.0), axis=2)]
  transfers between devices with their start and end apart: 8 -> 0, of which waited for: 8 -> 0; matrix products, arithmetic and copies ran while one was open for 6% -> 0% of each run, Pallas kernels for 0% -> 0%
where the time goes in v2:
time: 97.9 us; the launch traced here: 96.9 us
  Pallas kernels  96.3 us (98%)
    pallas_call x1, Pallas kernels, sliced(): pl.pallas_call(sliced_kernel, out_shape=(jax.ShapeDtypeStruct((1, rows),...  53.4 us
    pallas_call x1, Pallas kernels, sliced(): pl.pallas_call(joined_kernel, out_shape=(jax.ShapeDtypeStruct((1, rows),...  42.9 us

profile of v2, /device:TPU:0, one launch (start us, length us, event | category | flops | bytes accessed | tf_op | source)
XLA Modules:
  0.0 96.9 jit_solution(2449146124026289772)
XLA Ops:
  0.6 53.4 %sliced.1 = (f32[1,128]{1,0:T(1,128)}, bf16[4,128,1408]{2,1,0:T(8,128)(2,1)}, bf16[4,16,1408]{2,1,0:T(8,128)(2,1)}) custom-call(s32[4]{0:T(128)} %order_in.1, s32[1,128]{1,0:T(1,128)} %bitcast.6, s32[1,128]{1,0:T(1,128)} %bitcast.7, bf16[1,128]{1,0:T(2,128)(2,1)} %bitcast.8, bf16[128,5376]{1,0:T(8,128)(2,1)} %states.1, bf16[128,5376]{1,0:T(8,128)(2,1)} %bitcast.5), custom_call_target="tpu_custom_call" | custom-call | tf_op jit(solution)/shard_map/sliced/pallas_call | solution.py:339
  54.0 42.9 %joined.1 = (f32[1,128]{1,0:T(1,128)}, bf16[128,5376]{1,0:T(8,128)(2,1)}, f32[1,16,5376]{2,1,0:T(8,128)}) custom-call(f32[1,128]{1,0:T(1,128)} %get-tuple-element.9.loss_in, bf16[4,128,1408]{2,1,0:T(8,128)(2,1)} %get-tuple-element.10.back_in, bf16[4,16,1408]{2,1,0:T(8,128)(2,1)} %get-tuple-element.11.head_in), custom_call_target="tpu_custom_call" | custom-call | tf_op jit(solution)/shard_map/joined/pallas_call | solution.py:383

commit v3 on v2

--- a/solution.py
+++ b/solution.py
@@ -300,29 +300,39 @@
         copy.wait_send()
 
 
-def joined_kernel(loss_in, back_in, head_in, loss_out, state_out, head_out, head_got, head_done, sems):
+def joined_kernel(
+    loss_in, back_in, head_in, loss_out, state_out, head_out, loss_got, back_got, head_got, head_done, got, put
+):
     wide = back_in.shape[2]
     over = LANGS * wide - state_out.shape[1]
-    fetch = pltpu.make_async_copy(head_in, head_got, sems.at[0])
-    fetch.start()
-    copies = [pltpu.make_async_copy(loss_in, loss_out, sems.at[1])]
-    for e in range(LANGS):
-        skip = over if e == LANGS - 1 else 0
-        here = pl.ds(e * wide, wide - skip)
-        copies.append(
-            pltpu.make_async_copy(back_in.at[e, :, pl.ds(skip, wide - skip)], state_out.at[:, here], sems.at[2 + e])
-        )
-    for copy in copies:
-        copy.start()
-    fetch.wait()
-    for e in range(LANGS):
-        skip = over if e == LANGS - 1 else 0
+    loads = [
+        pltpu.make_async_copy(head_in, head_got, got.at[LANGS]),
+        pltpu.make_async_copy(loss_in, loss_got, got.at[LANGS + 1]),
+    ]
+    loads += [pltpu.make_async_copy(back_in.at[e], back_got.at[e], got.at[e]) for e in range(LANGS)]
+    for copy in loads:
+        copy.start()
+    skips = [over if e == LANGS - 1 else 0 for e in range(LANGS)]
+    stores = []
+
+    def store(src, dst, n):
+        copy = pltpu.make_async_copy(src, dst, put.at[n])
+        copy.start()
+        stores.append(copy)
+
+    loads[0].wait()
+    for e, skip in enumerate(skips):
         head_done[0, :, pl.ds(e * wide, wide - skip)] = head_got[e, :, pl.ds(skip, wide - skip)].astype(F32)
-    store = pltpu.make_async_copy(head_done, head_out, sems.at[2 + LANGS])
-    store.start()
-    for copy in copies:
+    store(head_done, head_out, LANGS)
+    loads[1].wait()
+    store(loss_got, loss_out, LANGS + 1)
+    for e, skip in enumerate(skips):
+        loads[2 + e].wait()
+        store(
+            back_got.at[e, :, pl.ds(skip, wide - skip)], state_out.at[:, pl.ds(e * wide, wide - skip)], e
+        )
+    for copy in stores:
         copy.wait()
-    store.wait()
 
 
 def sliced(final_states, head_blocks, block_order, row_tags, target_word, row_weight):
@@ -390,9 +400,12 @@
         in_specs=[hbm] * 3,
         out_specs=[hbm] * 3,
         scratch_shapes=[
+            pltpu.VMEM((1, rows), F32),
+            pltpu.VMEM((LANGS, rows, wide), BF16),
             pltpu.VMEM((LANGS, share, wide), BF16),
             pltpu.VMEM((1, share, width), F32),
-            dma((LANGS + 3,)),
+            dma((LANGS + 2,)),
+            dma((LANGS + 2,)),
         ],
         compiler_params=pltpu.CompilerParams(vmem_limit_bytes=60 * 1024 * 1024),
         name="joined",

time: 97.9 us -> 57.3 us (0.59)
  Pallas kernels: 96.3 us -> 55.7 us
    pallas_call x1, Pallas kernels: 42.9 us -> 2.26 us  [sliced(): pl.pallas_call(joined_kernel, out_shape=(jax.ShapeDtypeStruct((1, rows),...]
where the time goes in v3:
time: 57.3 us; the launch traced here: 56.3 us
  Pallas kernels  55.7 us (97%)
  between operations  0.64 us (1%)
    pallas_call x1, Pallas kernels, sliced(): pl.pallas_call(sliced_kernel, out_shape=(jax.ShapeDtypeStruct((1, rows),...  53.4 us
    pallas_call x1, Pallas kernels, sliced(): pl.pallas_call(joined_kernel, out_shape=(jax.ShapeDtypeStruct((1, rows),...  2.26 us

profile of v3, /device:TPU:0, one launch (start us, length us, event | category | flops | bytes accessed | tf_op | source)
XLA Modules:
  0.0 56.3 jit_solution(13473937746155073380)
XLA Ops:
  0.6 53.4 %sliced.1 = (f32[1,128]{1,0:T(1,128)}, bf16[4,128,1408]{2,1,0:T(8,128)(2,1)}, bf16[4,16,1408]{2,1,0:T(8,128)(2,1)}) custom-call(s32[4]{0:T(128)} %order_in.1, s32[1,128]{1,0:T(1,128)} %bitcast.6, s32[1,128]{1,0:T(1,128)} %bitcast.7, bf16[1,128]{1,0:T(2,128)(2,1)} %bitcast.8, bf16[128,5376]{1,0:T(8,128)(2,1)} %states.1, bf16[128,5376]{1,0:T(8,128)(2,1)} %bitcast.5), custom_call_target="tpu_custom_call" | custom-call | tf_op jit(solution)/shard_map/sliced/pallas_call | solution.py:349
  54.0 2.3 %joined.1 = (f32[1,128]{1,0:T(1,128)}, bf16[128,5376]{1,0:T(8,128)(2,1)}, f32[1,16,5376]{2,1,0:T(8,128)}) custom-call(f32[1,128]{1,0:T(1,128)} %get-tuple-element.9.loss_in, bf16[4,128,1408]{2,1,0:T(8,128)(2,1)} %get-tuple-element.10.back_in, bf16[4,16,1408]{2,1,0:T(8,128)(2,1)} %get-tuple-element.11.head_in), custom_call_target="tpu_custom_call" | custom-call | tf_op jit(solution)/shard_map/joined/pallas_call | solution.py:393

commit v4 on v3

--- a/solution.py
+++ b/solution.py
@@ -238,7 +238,12 @@
         return pl.ds(pl.multiple_of(2 * share * e + share * which, 16), share)
 
     pair_copies = {}
-    for d in (2, 1, 3, 0):
+    line_copies = []
+
+    def both(d, e):
+        return term[d, mine_of(e, core), :] + pair_got[d, pl.ds(e * share, share), :].astype(F32)
+
+    def head_term(d):
         picked = spread[:, pl.ds(pl.multiple_of(planes[d] * BLOCK, 128), BLOCK)]
         term[d] = dot(picked, cols[...], (0, 0))
         for e in range(LANGS):
@@ -246,12 +251,7 @@
         pair_copies[d] = remote(pair_send.at[d], pair_got.at[d], pair_s.at[d], pair_r.at[d], twin)
         pair_copies[d].start()
 
-    line_copies = []
-
-    def both(d, e):
-        return term[d, mine_of(e, core), :] + pair_got[d, pl.ds(e * share, share), :].astype(F32)
-
-    for d in (2, 1, 3):
+    def along_line(d):
         pair_copies[d].wait_recv()
         for e in range(LANGS):
             line_send[d - 1, pl.ds(e * share, share), :] = both(d, e).astype(BF16)
@@ -261,8 +261,15 @@
         copy.start()
         line_copies.append(copy)
 
+    head_term(2)
+    head_term(1)
+    along_line(2)
+    head_term(3)
+    along_line(1)
+    along_line(3)
     for b in range(1, BATCHES):
         give_back(b)
+    head_term(0)
 
     loss = jnp.concatenate(losses, axis=0)
     loss_out[...] = jnp.sum(jnp.where(square, loss, 0.0), axis=0, keepdims=True)

time: 57.3 us -> 57 us (level)
  no operation moved by 1% of the time
where the time goes in v4:
time: 57 us; the launch traced here: 56.3 us
  Pallas kernels  55.7 us (98%)
  between operations  0.64 us (1%)
    pallas_call x1, Pallas kernels, sliced(): pl.pallas_call(sliced_kernel, out_shape=(jax.ShapeDtypeStruct((1, rows),...  53.4 us
    pallas_call x1, Pallas kernels, sliced(): pl.pallas_call(joined_kernel, out_shape=(jax.ShapeDtypeStruct((1, rows),...  2.26 us

profile of v4, /device:TPU:0, one launch (start us, length us, event | category | flops | bytes accessed | tf_op | source)
XLA Modules:
  0.0 56.3 jit_solution(373709331400788878)
XLA Ops:
  0.6 53.4 %sliced.1 = (f32[1,128]{1,0:T(1,128)}, bf16[4,128,1408]{2,1,0:T(8,128)(2,1)}, bf16[4,16,1408]{2,1,0:T(8,128)(2,1)}) custom-call(s32[4]{0:T(128)} %order_in.1, s32[1,128]{1,0:T(1,128)} %bitcast.6, s32[1,128]{1,0:T(1,128)} %bitcast.7, bf16[1,128]{1,0:T(2,128)(2,1)} %bitcast.8, bf16[128,5376]{1,0:T(8,128)(2,1)} %states.1, bf16[128,5376]{1,0:T(8,128)(2,1)} %bitcast.5), custom_call_target="tpu_custom_call" | custom-call | tf_op jit(solution)/shard_map/sliced/pallas_call | solution.py:356
  54.1 2.3 %joined.1 = (f32[1,128]{1,0:T(1,128)}, bf16[128,5376]{1,0:T(8,128)(2,1)}, f32[1,16,5376]{2,1,0:T(8,128)}) custom-call(f32[1,128]{1,0:T(1,128)} %get-tuple-element.9.loss_in, bf16[4,128,1408]{2,1,0:T(8,128)(2,1)} %get-tuple-element.10.back_in, bf16[4,16,1408]{2,1,0:T(8,128)(2,1)} %get-tuple-element.11.head_in), custom_call_target="tpu_custom_call" | custom-call | tf_op jit(solution)/shard_map/joined/pallas_call | solution.py:400

commit v5 on v4

--- a/solution.py
+++ b/solution.py
@@ -30,7 +30,7 @@
     loss_out, back_out, head_out,
     order, tags, words, weights, cols, head, owner, part_send, part_got, grads, spread,
     back_send, term, pair_send, pair_got, line_send, line_got, plane_send,
-    small_s, own_s, tag_s, tag_r, head_s, head_r, twin_s, twin_r, row_s, row_r,
+    small_s, own_s, tag_s, tag_r, up_s, up_r, down_s, down_r, twin_s, twin_r, row_s, row_r,
     part_s, part_r, grad_s, grad_r, back_s, back_r, pair_s, pair_r, line_s, line_r, plane_s, plane_r,
 ):
     rows, width = states.shape
@@ -85,15 +85,35 @@
 
     pl.semaphore_wait(barrier, len(friends))
 
-    head_copies = []
-    for d in (2, 1, 3):
-        copy = remote(
-            block.at[pl.ds(pl.multiple_of(half * core, 16), half), features(own)],
-            head.at[words_at(z, half * core, half), :],
-            head_s.at[d - 1], head_r.at[d - 1], (dp, planes[d]),
-        )
-        copy.start()
-        head_copies.append(copy)
+    def half_at(plane_id, which):
+        return head.at[words_at(plane_id, half * which, half), :]
+
+    own_half = block.at[pl.ds(pl.multiple_of(half * core, 16), half), features(own)]
+    above, below = (dp, planes[1]), (dp, planes[LANGS - 1])
+
+    def upward(k):
+        src = half_at(sources[k], core) if k else own_half
+        return remote(src, half_at(sources[k], core), up_s.at[k], up_r.at[k], above)
+
+    def downward(k):
+        src = half_at(planes[k], core) if k else own_half
+        return remote(src, half_at(planes[k], core), down_s.at[k], down_r.at[k], below)
+
+    def twin_up(k):
+        return remote(half_at(sources[k], core), half_at(sources[k], core), twin_s.at[k], twin_r.at[k], twin)
+
+    def twin_down(k):
+        return remote(
+            half_at(planes[k], core), half_at(planes[k], core), twin_s.at[LANGS + k], twin_r.at[LANGS + k], twin
+        )
+
+    last = LANGS - 1
+
+    def when(condition, act):
+        pl.when(condition)(act)
+
+    when(z < last, lambda: upward(0).start())
+    when(z > 0, lambda: downward(0).start())
     tag_copies = []
     for r in (3, 1, 2):
         copy = remote(tags_in, tags.at[r], tag_s.at[r - 1], tag_r.at[r - 1], plane[r])
@@ -133,22 +153,24 @@
     target = column(words[...].astype(F32)).astype(jnp.int32)
     weight = column(weights[...].astype(F32))
 
-    twin_copies = []
-    for d in (1, 2, 3):
-        remote(
-            head.at[words_at(sources[d], half * core, half), :],
-            head.at[words_at(sources[d], half * core, half), :],
-            head_s.at[d - 1], head_r.at[d - 1], (dp, planes[d]),
-        ).wait_recv()
-        copy = remote(
-            head.at[words_at(sources[d], half * core, half), :],
-            head.at[words_at(sources[d], half * core, half), :],
-            twin_s.at[d - 1], twin_r.at[d - 1], twin,
-        )
-        copy.start()
-        twin_copies.append(copy)
-    for copy in twin_copies:
-        copy.wait_recv()
+    for k in range(1, LANGS):
+        @pl.when(z >= k)
+        def _(k=k):
+            upward(k - 1).wait_recv()
+            if k < last:
+                when(z < last, lambda: upward(k).start())
+            twin_up(k).start()
+
+        @pl.when(z + k <= last)
+        def _(k=k):
+            downward(k - 1).wait_recv()
+            if k < last:
+                when(z > 0, lambda: downward(k).start())
+            twin_down(k).start()
+
+    for k in range(1, LANGS):
+        when(z >= k, lambda k=k: twin_up(k).wait_recv())
+        when(z + k <= last, lambda k=k: twin_down(k).wait_recv())
     mine[0].wait()
 
     part_copies = [[] for _ in range(BATCHES)]
@@ -298,8 +320,14 @@
         copy.wait_recv()
     for copy in mine[1 + BATCHES :]:
         copy.wait()
+    for k in range(LANGS - 1):
+        when((z >= k) & (z < last), lambda k=k: upward(k).wait_send())
+        when((z + k <= last) & (z > 0), lambda k=k: downward(k).wait_send())
+    for k in range(1, LANGS):
+        when(z >= k, lambda k=k: twin_up(k).wait_send())
+        when(z + k <= last, lambda k=k: twin_down(k).wait_send())
     everything = (
-        head_copies + tag_copies + twin_copies + back_copies + line_copies + plane_copies
+        tag_copies + back_copies + line_copies + plane_copies
         + [c for group in row_copies + part_copies + grad_copies for c in group]
         + [pair_copies[d] for d in range(LANGS)]
     )
@@ -381,7 +409,8 @@
             pltpu.VMEM((LANGS - 1, half, wide), BF16),
             pltpu.VMEM((LANGS - 1, half, wide), BF16),
             pltpu.VMEM((LANGS, share, wide), BF16),
-            dma((4,)), dma((2 * BATCHES + 2,)), three, three, three, three, three, three, batches, batches,
+            dma((4,)), dma((2 * BATCHES + 2,)), three, three, three, three, three, three,
+            dma((2 * LANGS,)), dma((2 * LANGS,)), batches, batches,
             batches, batches, batches, batches, batches, batches, dma((LANGS,)), dma((LANGS,)),
             three, three, three, three,
         ],

time: 57 us -> 58.1 us (1.019)
  Pallas kernels: 55.7 us -> 57.3 us
    pallas_call x1, Pallas kernels: 53.4 us -> 55.1 us  [sliced(): pl.pallas_call(sliced_kernel, out_shape=(jax.ShapeDtypeStruct((1, rows),...]
where the time goes in v5:
time: 58.1 us; the launch traced here: 58 us
  Pallas kernels  57.3 us (99%)
  between operations  0.64 us (1%)
    pallas_call x1, Pallas kernels, sliced(): pl.pallas_call(sliced_kernel, out_shape=(jax.ShapeDtypeStruct((1, rows),...  55.1 us
    pallas_call x1, Pallas kernels, sliced(): pl.pallas_call(joined_kernel, out_shape=(jax.ShapeDtypeStruct((1, rows),...  2.26 us

profile of v5, /device:TPU:0, one launch (start us, length us, event | category | flops | bytes accessed | tf_op | source)
XLA Modules:
  0.0 58.0 jit_solution(2708602451607494219)
XLA Ops:
  0.6 55.1 %sliced.1 = (f32[1,128]{1,0:T(1,128)}, bf16[4,128,1408]{2,1,0:T(8,128)(2,1)}, bf16[4,16,1408]{2,1,0:T(8,128)(2,1)}) custom-call(s32[4]{0:T(128)} %order_in.1, s32[1,128]{1,0:T(1,128)} %bitcast.6, s32[1,128]{1,0:T(1,128)} %bitcast.7, bf16[1,128]{1,0:T(2,128)(2,1)} %bitcast.8, bf16[128,5376]{1,0:T(8,128)(2,1)} %states.1, bf16[128,5376]{1,0:T(8,128)(2,1)} %bitcast.5), custom_call_target="tpu_custom_call" | custom-call | tf_op jit(solution)/shard_map/sliced/pallas_call | solution.py:384
  55.7 2.3 %joined.1 = (f32[1,128]{1,0:T(1,128)}, bf16[128,5376]{1,0:T(8,128)(2,1)}, f32[1,16,5376]{2,1,0:T(8,128)}) custom-call(f32[1,128]{1,0:T(1,128)} %get-tuple-element.9.loss_in, bf16[4,128,1408]{2,1,0:T(8,128)(2,1)} %get-tuple-element.10.back_in, bf16[4,16,1408]{2,1,0:T(8,128)(2,1)} %get-tuple-element.11.head_in), custom_call_target="tpu_custom_call" | custom-call | tf_op jit(solution)/shard_map/joined/pallas_call | solution.py:429

commit v6 on v4

--- a/solution.py
+++ b/solution.py
@@ -99,8 +99,9 @@
         copy = remote(tags_in, tags.at[r], tag_s.at[r - 1], tag_r.at[r - 1], plane[r])
         copy.start()
         tag_copies.append(copy)
-    row_copies = [[], []]
-    for b in range(BATCHES):
+    row_copies = [[] for _ in range(BATCHES)]
+
+    def send_rows(b):
         for r in (3, 1, 2):
             n = b * 3 + r - 1
             copy = remote(
@@ -111,6 +112,7 @@
             copy.start()
             row_copies[b].append(copy)
 
+    send_rows(0)
     for copy in small:
         copy.wait()
     square = iota((rows, rows), 0) == iota((rows, rows), 1)
@@ -132,6 +134,10 @@
             owner[span(b, r), :] = number[b * batch : (b + 1) * batch]
     target = column(words[...].astype(F32)).astype(jnp.int32)
     weight = column(weights[...].astype(F32))
+
+    for copy in row_copies[0]:
+        copy.wait_send()
+    send_rows(1)
 
     twin_copies = []
     for d in (1, 2, 3):
@@ -225,14 +231,13 @@
         copy.start()
         mine.append(copy)
 
-    for b in range(BATCHES):
-        partial_logits(b)
-    for b in range(BATCHES):
-        softmax_grads(b)
-    for b in range(BATCHES):
-        spread_grads(b)
-        if b == 0:
-            give_back(0)
+    partial_logits(0)
+    softmax_grads(0)
+    partial_logits(1)
+    spread_grads(0)
+    give_back(0)
+    softmax_grads(1)
+    spread_grads(1)
 
     def mine_of(e, which):
         return pl.ds(pl.multiple_of(2 * share * e + share * which, 16), share)
@@ -300,7 +305,7 @@
         copy.wait()
     everything = (
         head_copies + tag_copies + twin_copies + back_copies + line_copies + plane_copies
-        + [c for group in row_copies + part_copies + grad_copies for c in group]
+        + [c for group in row_copies[1:] + part_copies + grad_copies for c in group]
         + [pair_copies[d] for d in range(LANGS)]
     )
     for copy in everything:

time: 57 us -> 65.7 us (1.15)
  Pallas kernels: 55.7 us -> 64.9 us
    pallas_call x1, Pallas kernels: 53.4 us -> 62.6 us  [sliced(): pl.pallas_call(sliced_kernel, out_shape=(jax.ShapeDtypeStruct((1, rows),...]
where the time goes in v6:
time: 65.7 us; the launch traced here: 65.5 us
  Pallas kernels  64.9 us (99%)
    pallas_call x1, Pallas kernels, sliced(): pl.pallas_call(sliced_kernel, out_shape=(jax.ShapeDtypeStruct((1, rows),...  62.6 us
    pallas_call x1, Pallas kernels, sliced(): pl.pallas_call(joined_kernel, out_shape=(jax.ShapeDtypeStruct((1, rows),...  2.26 us

profile of v6, /device:TPU:0, one launch (start us, length us, event | category | flops | bytes accessed | tf_op | source)
XLA Modules:
  0.0 65.5 jit_solution(16132243783961584685)
XLA Ops:
  0.6 62.6 %sliced.1 = (f32[1,128]{1,0:T(1,128)}, bf16[4,128,1408]{2,1,0:T(8,128)(2,1)}, bf16[4,16,1408]{2,1,0:T(8,128)(2,1)}) custom-call(s32[4]{0:T(128)} %order_in.1, s32[1,128]{1,0:T(1,128)} %bitcast.6, s32[1,128]{1,0:T(1,128)} %bitcast.7, bf16[1,128]{1,0:T(2,128)(2,1)} %bitcast.8, bf16[128,5376]{1,0:T(8,128)(2,1)} %states.1, bf16[128,5376]{1,0:T(8,128)(2,1)} %bitcast.5), custom_call_target="tpu_custom_call" | custom-call | tf_op jit(solution)/shard_map/sliced/pallas_call | solution.py:361
  63.3 2.3 %joined.1 = (f32[1,128]{1,0:T(1,128)}, bf16[128,5376]{1,0:T(8,128)(2,1)}, f32[1,16,5376]{2,1,0:T(8,128)}) custom-call(f32[1,128]{1,0:T(1,128)} %get-tuple-element.9.loss_in, bf16[4,128,1408]{2,1,0:T(8,128)(2,1)} %get-tuple-element.10.back_in, bf16[4,16,1408]{2,1,0:T(8,128)(2,1)} %get-tuple-element.11.head_in), custom_call_target="tpu_custom_call" | custom-call | tf_op jit(solution)/shard_map/joined/pallas_call | solution.py:405

commit v7 on v4

--- a/solution.py
+++ b/solution.py
@@ -231,8 +231,6 @@
         softmax_grads(b)
     for b in range(BATCHES):
         spread_grads(b)
-        if b == 0:
-            give_back(0)
 
     def mine_of(e, which):
         return pl.ds(pl.multiple_of(2 * share * e + share * which, 16), share)
@@ -267,7 +265,7 @@
     head_term(3)
     along_line(1)
     along_line(3)
-    for b in range(1, BATCHES):
+    for b in range(BATCHES):
         give_back(b)
     head_term(0)
 

time: 57 us -> 58.4 us (1.025)
  Pallas kernels: 55.7 us -> 57.6 us
    pallas_call x1, Pallas kernels: 53.4 us -> 55.4 us  [sliced(): pl.pallas_call(sliced_kernel, out_shape=(jax.ShapeDtypeStruct((1, rows),...]
where the time goes in v7:
time: 58.4 us; the launch traced here: 58.3 us
  Pallas kernels  57.6 us (99%)
  between operations  0.64 us (1%)
    pallas_call x1, Pallas kernels, sliced(): pl.pallas_call(sliced_kernel, out_shape=(jax.ShapeDtypeStruct((1, rows),...  55.4 us
    pallas_call x1, Pallas kernels, sliced(): pl.pallas_call(joined_kernel, out_shape=(jax.ShapeDtypeStruct((1, rows),...  2.26 us

profile of v7, /device:TPU:0, one launch (start us, length us, event | category | flops | bytes accessed | tf_op | source)
XLA Modules:
  0.0 58.3 jit_solution(8711384414359730305)
XLA Ops:
  0.6 55.4 %sliced.1 = (f32[1,128]{1,0:T(1,128)}, bf16[4,128,1408]{2,1,0:T(8,128)(2,1)}, bf16[4,16,1408]{2,1,0:T(8,128)(2,1)}) custom-call(s32[4]{0:T(128)} %order_in.1, s32[1,128]{1,0:T(1,128)} %bitcast.6, s32[1,128]{1,0:T(1,128)} %bitcast.7, bf16[1,128]{1,0:T(2,128)(2,1)} %bitcast.8, bf16[128,5376]{1,0:T(8,128)(2,1)} %states.1, bf16[128,5376]{1,0:T(8,128)(2,1)} %bitcast.5), custom_call_target="tpu_custom_call" | custom-call | tf_op jit(solution)/shard_map/sliced/pallas_call | solution.py:354
  56.0 2.3 %joined.1 = (f32[1,128]{1,0:T(1,128)}, bf16[128,5376]{1,0:T(8,128)(2,1)}, f32[1,16,5376]{2,1,0:T(8,128)}) custom-call(f32[1,128]{1,0:T(1,128)} %get-tuple-element.9.loss_in, bf16[4,128,1408]{2,1,0:T(8,128)(2,1)} %get-tuple-element.10.back_in, bf16[4,16,1408]{2,1,0:T(8,128)(2,1)} %get-tuple-element.11.head_in), custom_call_target="tpu_custom_call" | custom-call | tf_op jit(solution)/shard_map/joined/pallas_call | solution.py:398

commit v8 on v4

--- a/solution.py
+++ b/solution.py
@@ -65,6 +65,14 @@
     def words_at(plane_id, first, count):
         return pl.ds(pl.multiple_of(plane_id * BLOCK + first, 16), count)
 
+    turns = []
+    for r in (jnp.int32(3), 1 + core, 2 - core):
+        chip = lax.rem(y + lax.div(r, 2), 2) * 2 + lax.rem(x + lax.rem(r, 2), 2)
+        turns.append((r, chip, (chip * 2 + core, z)))
+
+    def spot(b, r):
+        return pl.ds(pl.multiple_of((b * 4 + r) * batch, batch), batch)
+
     barrier = pltpu.get_barrier_semaphore()
     friends = plane[1:] + [(dp, planes[d]) for d in range(1, LANGS)] + [twin]
     for friend in friends:
@@ -101,12 +109,12 @@
         tag_copies.append(copy)
     row_copies = [[], []]
     for b in range(BATCHES):
-        for r in (3, 1, 2):
+        for r, chip, to in turns:
             n = b * 3 + r - 1
             copy = remote(
-                states.at[pl.ds(b * batch, batch), features(chips[r])],
-                cols.at[span(b, r), :],
-                row_s.at[n], row_r.at[n], plane[r],
+                states.at[pl.ds(b * batch, batch), features(chip)],
+                cols.at[spot(b, r), :],
+                row_s.at[n], row_r.at[n], to,
             )
             copy.start()
             row_copies[b].append(copy)
@@ -210,12 +218,12 @@
 
     def give_back(b):
         back_send[whole(b), :] = dot(spread[whole(b), :], head[...], (1, 0)).astype(BF16)
-        for r in (3, 1, 2):
+        for r, _, to in turns:
             n = b * 3 + r - 1
             copy = remote(
-                back_send.at[span(b, r), :],
+                back_send.at[spot(b, r), :],
                 back_out.at[own, pl.ds(b * batch, batch), :],
-                back_s.at[n], back_r.at[n], plane[r],
+                back_s.at[n], back_r.at[n], to,
             )
             copy.start()
             back_copies.append(copy)

time: 57 us -> 57 us (level)
  no operation moved by 1% of the time
where the time goes in v8:
time: 57 us; the launch traced here: 56.3 us
  Pallas kernels  55.7 us (98%)
  between operations  0.64 us (1%)
    pallas_call x1, Pallas kernels, sliced(): pl.pallas_call(sliced_kernel, out_shape=(jax.ShapeDtypeStruct((1, rows),...  53.4 us
    pallas_call x1, Pallas kernels, sliced(): pl.pallas_call(joined_kernel, out_shape=(jax.ShapeDtypeStruct((1, rows),...  2.26 us

profile of v8, /device:TPU:0, one launch (start us, length us, event | category | flops | bytes accessed | tf_op | source)
XLA Modules:
  0.0 56.3 jit_solution(6737823028963067089)
XLA Ops:
  0.6 53.4 %sliced.1 = (f32[1,128]{1,0:T(1,128)}, bf16[4,128,1408]{2,1,0:T(8,128)(2,1)}, bf16[4,16,1408]{2,1,0:T(8,128)(2,1)}) custom-call(s32[4]{0:T(128)} %order_in.1, s32[1,128]{1,0:T(1,128)} %bitcast.6, s32[1,128]{1,0:T(1,128)} %bitcast.7, bf16[1,128]{1,0:T(2,128)(2,1)} %bitcast.8, bf16[128,5376]{1,0:T(8,128)(2,1)} %states.1, bf16[128,5376]{1,0:T(8,128)(2,1)} %bitcast.5), custom_call_target="tpu_custom_call" | custom-call | tf_op jit(solution)/shard_map/sliced/pallas_call | solution.py:364
  54.1 2.3 %joined.1 = (f32[1,128]{1,0:T(1,128)}, bf16[128,5376]{1,0:T(8,128)(2,1)}, f32[1,16,5376]{2,1,0:T(8,128)}) custom-call(f32[1,128]{1,0:T(1,128)} %get-tuple-element.9.loss_in, bf16[4,128,1408]{2,1,0:T(8,128)(2,1)} %get-tuple-element.10.back_in, bf16[4,16,1408]{2,1,0:T(8,128)(2,1)} %get-tuple-element.11.head_in), custom_call_target="tpu_custom_call" | custom-call | tf_op jit(solution)/shard_map/joined/pallas_call | solution.py:408

commit v9 on v7

--- a/solution.py
+++ b/solution.py
@@ -10,7 +10,7 @@
 MESH = pl.DeviceIdType.MESH
 F32 = jnp.float32
 BF16 = jnp.bfloat16
-BATCHES = 2
+BATCHES = 1
 
 
 def dot(a, b, dims):
@@ -99,7 +99,7 @@
         copy = remote(tags_in, tags.at[r], tag_s.at[r - 1], tag_r.at[r - 1], plane[r])
         copy.start()
         tag_copies.append(copy)
-    row_copies = [[], []]
+    row_copies = [{} for _ in range(BATCHES)]
     for b in range(BATCHES):
         for r in (3, 1, 2):
             n = b * 3 + r - 1
@@ -109,7 +109,7 @@
                 row_s.at[n], row_r.at[n], plane[r],
             )
             copy.start()
-            row_copies[b].append(copy)
+            row_copies[b][r] = copy
 
     for copy in small:
         copy.wait()
@@ -152,35 +152,35 @@
     mine[0].wait()
 
     part_copies = [[] for _ in range(BATCHES)]
-    grad_copies = [[] for _ in range(BATCHES)]
+    grad_copies = [{} for _ in range(BATCHES)]
     back_copies = []
     losses = []
 
-    def whole(b):
-        return pl.ds(b * 4 * batch, 4 * batch)
-
-    def partial_logits(b):
-        mine[1 + b].wait()
-        for copy in row_copies[b]:
-            copy.wait_recv()
+    def partial_logits(b, r):
+        here = span(b, r)
+        if r:
+            row_copies[b][r].wait_recv()
+        else:
+            mine[1 + b].wait()
 
         if over:
             @pl.when(own == LANGS - 1)
             def _():
-                cols[whole(b), :over] = jnp.zeros((4 * batch, over), BF16)
-
-        every = dot(cols[whole(b), :], head[...], (1, 1))
-        number = owner[whole(b), :]
-        kept = jnp.zeros((4 * batch, BLOCK), F32)
+                cols[here, :over] = jnp.zeros((batch, over), BF16)
+
+        every = dot(cols[here, :], head[...], (1, 1))
+        number = owner[here, :]
+        kept = jnp.zeros((batch, BLOCK), F32)
         for n in range(LANGS):
             kept = jnp.where(number == n, every[:, n * BLOCK : (n + 1) * BLOCK], kept)
-        part_got[span(b, 0), :] = kept[:batch]
-        for r in (3, 1, 2):
-            n = b * 3 + r - 1
-            part_send[span(b, r), :] = kept[r * batch : (r + 1) * batch]
-            copy = remote(part_send.at[span(b, r), :], part_got.at[span(b, r), :], part_s.at[n], part_r.at[n], plane[r])
-            copy.start()
-            part_copies[b].append(copy)
+        if r == 0:
+            part_got[here, :] = kept
+            return
+        n = b * 3 + r - 1
+        part_send[here, :] = kept
+        copy = remote(part_send.at[here, :], part_got.at[here, :], part_s.at[n], part_r.at[n], plane[r])
+        copy.start()
+        part_copies[b].append(copy)
 
     def softmax_grads(b):
         for copy in part_copies[b]:
@@ -198,39 +198,40 @@
             n = b * 3 + r - 1
             copy = remote(grads.at[span(b, 0), :], grads.at[span(b, r), :], grad_s.at[n], grad_r.at[n], plane[r])
             copy.start()
-            grad_copies[b].append(copy)
-
-    def spread_grads(b):
-        for copy in grad_copies[b]:
-            copy.wait_recv()
-        number = owner[whole(b), :]
-        values = grads[whole(b), :].astype(F32)
+            grad_copies[b][r] = copy
+
+    def spread_grads(b, r):
+        here = span(b, r)
+        if r:
+            grad_copies[b][r].wait_recv()
+        number = owner[here, :]
+        values = grads[here, :].astype(F32)
         for n in range(LANGS):
-            spread[whole(b), pl.ds(n * BLOCK, BLOCK)] = jnp.where(number == n, values, 0.0).astype(BF16)
-
-    def give_back(b):
-        back_send[whole(b), :] = dot(spread[whole(b), :], head[...], (1, 0)).astype(BF16)
-        for r in (3, 1, 2):
+            spread[here, pl.ds(n * BLOCK, BLOCK)] = jnp.where(number == n, values, 0.0).astype(BF16)
+
+    def give_back(b, r):
+        here = span(b, r)
+        back_send[here, :] = dot(spread[here, :], head[...], (1, 0)).astype(BF16)
+        there = back_out.at[own, pl.ds(b * batch, batch), :]
+        if r:
             n = b * 3 + r - 1
-            copy = remote(
-                back_send.at[span(b, r), :],
-                back_out.at[own, pl.ds(b * batch, batch), :],
-                back_s.at[n], back_r.at[n], plane[r],
-            )
-            copy.start()
+            copy = remote(back_send.at[here, :], there, back_s.at[n], back_r.at[n], plane[r])
             back_copies.append(copy)
-        copy = pltpu.make_async_copy(
-            back_send.at[span(b, 0), :], back_out.at[own, pl.ds(b * batch, batch), :], own_s.at[BATCHES + 1 + b]
-        )
-        copy.start()
-        mine.append(copy)
+        else:
+            copy = pltpu.make_async_copy(back_send.at[here, :], there, own_s.at[BATCHES + 1 + b])
+            mine.append(copy)
+        copy.start()
 
     for b in range(BATCHES):
-        partial_logits(b)
+        for r in (3, 1, 2, 0):
+            partial_logits(b, r)
     for b in range(BATCHES):
         softmax_grads(b)
     for b in range(BATCHES):
-        spread_grads(b)
+        for r in (3, 1, 2, 0):
+            spread_grads(b, r)
+            if r in (3, 1):
+                give_back(b, r)
 
     def mine_of(e, which):
         return pl.ds(pl.multiple_of(2 * share * e + share * which, 16), share)
@@ -266,7 +267,8 @@
     along_line(1)
     along_line(3)
     for b in range(BATCHES):
-        give_back(b)
+        give_back(b, 2)
+        give_back(b, 0)
     head_term(0)
 
     loss = jnp.concatenate(losses, axis=0)
@@ -298,7 +300,8 @@
         copy.wait()
     everything = (
         head_copies + tag_copies + twin_copies + back_copies + line_copies + plane_copies
-        + [c for group in row_copies + part_copies + grad_copies for c in group]
+        + [c for group in part_copies for c in group]
+        + [c for group in row_copies + grad_copies for c in group.values()]
         + [pair_copies[d] for d in range(LANGS)]
     )
     for copy in everything:

time: 58.4 us -> 58 us (level)
  no operation moved by 1% of the time
where the time goes in v9:
time: 58 us; the launch traced here: 57.8 us
  Pallas kernels  57.2 us (99%)
  between operations  0.64 us (1%)
    pallas_call x1, Pallas kernels, sliced(): pl.pallas_call(sliced_kernel, out_shape=(jax.ShapeDtypeStruct((1, rows),...  54.9 us
    pallas_call x1, Pallas kernels, sliced(): pl.pallas_call(joined_kernel, out_shape=(jax.ShapeDtypeStruct((1, rows),...  2.26 us

profile of v9, /device:TPU:0, one launch (start us, length us, event | category | flops | bytes accessed | tf_op | source)
XLA Modules:
  0.0 57.8 jit_solution(17104427747399610053)
XLA Ops:
  0.6 54.9 %sliced.1 = (f32[1,128]{1,0:T(1,128)}, bf16[4,128,1408]{2,1,0:T(8,128)(2,1)}, bf16[4,16,1408]{2,1,0:T(8,128)(2,1)}) custom-call(s32[4]{0:T(128)} %order_in.1, s32[1,128]{1,0:T(1,128)} %bitcast.6, s32[1,128]{1,0:T(1,128)} %bitcast.7, bf16[1,128]{1,0:T(2,128)(2,1)} %bitcast.8, bf16[128,5376]{1,0:T(8,128)(2,1)} %states.1, bf16[128,5376]{1,0:T(8,128)(2,1)} %bitcast.5), custom_call_target="tpu_custom_call" | custom-call | tf_op jit(solution)/shard_map/sliced/pallas_call | solution.py:357
  55.6 2.3 %joined.1 = (f32[1,128]{1,0:T(1,128)}, bf16[128,5376]{1,0:T(8,128)(2,1)}, f32[1,16,5376]{2,1,0:T(8,128)}) custom-call(f32[1,128]{1,0:T(1,128)} %get-tuple-element.9.loss_in, bf16[4,128,1408]{2,1,0:T(8,128)(2,1)} %get-tuple-element.10.back_in, bf16[4,16,1408]{2,1,0:T(8,128)(2,1)} %get-tuple-element.11.head_in), custom_call_target="tpu_custom_call" | custom-call | tf_op jit(solution)/shard_map/joined/pallas_call | solution.py:401

commit v10 on v4

--- a/solution.py
+++ b/solution.py
@@ -28,7 +28,7 @@
 def sliced_kernel(
     order_in, tags_in, words_in, weights_in, states, block,
     loss_out, back_out, head_out,
-    order, tags, words, weights, cols, head, owner, part_send, part_got, grads, spread,
+    order, tags, words, weights, loss_row, cols, head, owner, part_send, part_got, grads, spread,
     back_send, term, pair_send, pair_got, line_send, line_got, plane_send,
     small_s, own_s, tag_s, tag_r, head_s, head_r, twin_s, twin_r, row_s, row_r,
     part_s, part_r, grad_s, grad_r, back_s, back_r, pair_s, pair_r, line_s, line_r, plane_s, plane_r,
@@ -272,27 +272,29 @@
     head_term(0)
 
     loss = jnp.concatenate(losses, axis=0)
-    loss_out[...] = jnp.sum(jnp.where(square, loss, 0.0), axis=0, keepdims=True)
+    loss_row[...] = jnp.sum(jnp.where(square, loss, 0.0), axis=0, keepdims=True)
+    copy = pltpu.make_async_copy(loss_row, loss_out, own_s.at[2 * BATCHES + 2])
+    copy.start()
+    mine.append(copy)
 
     pair_copies[0].wait_recv()
     for copy in line_copies:
         copy.wait_recv()
-    for e in range(LANGS):
-        part = pl.ds(e * share, share)
-        plane_send[e] = (
-            (both(0, e) + line_got[0, part, :].astype(F32))
+    plane_copies = []
+    for r in (3, 1, 2, 0):
+        e = chips[r]
+        part = pl.ds(pl.multiple_of(e * share, share), share)
+        plane_send[r] = (
+            (term[0, mine_of(e, core), :] + pair_got[0, part, :].astype(F32) + line_got[0, part, :].astype(F32))
             + (line_got[1, part, :].astype(F32) + line_got[2, part, :].astype(F32))
         ).astype(BF16)
-    plane_copies = []
-    for r in (3, 1, 2):
-        copy = remote(
-            plane_send.at[chips[r]], head_out.at[own], plane_s.at[r - 1], plane_r.at[r - 1], plane[r]
-        )
-        copy.start()
-        plane_copies.append(copy)
-    copy = pltpu.make_async_copy(plane_send.at[own], head_out.at[own], own_s.at[2 * BATCHES + 1])
-    copy.start()
-    mine.append(copy)
+        if r:
+            copy = remote(plane_send.at[r], head_out.at[own], plane_s.at[r - 1], plane_r.at[r - 1], plane[r])
+            plane_copies.append(copy)
+        else:
+            copy = pltpu.make_async_copy(plane_send.at[0], head_out.at[own], own_s.at[2 * BATCHES + 1])
+            mine.append(copy)
+        copy.start()
 
     for copy in back_copies + plane_copies:
         copy.wait_recv()
@@ -316,7 +318,13 @@
         pltpu.make_async_copy(head_in, head_got, got.at[LANGS]),
         pltpu.make_async_copy(loss_in, loss_got, got.at[LANGS + 1]),
     ]
-    loads += [pltpu.make_async_copy(back_in.at[e], back_got.at[e], got.at[e]) for e in range(LANGS)]
+    piece = back_in.shape[1] // 2
+    pieces = [(e, h) for h in range(2) for e in range(LANGS)]
+    for e, h in pieces:
+        here = pl.ds(h * piece, piece)
+        loads.append(
+            pltpu.make_async_copy(back_in.at[e, here, :], back_got.at[e, here, :], got.at[LANGS + 2 + h * LANGS + e])
+        )
     for copy in loads:
         copy.start()
     skips = [over if e == LANGS - 1 else 0 for e in range(LANGS)]
@@ -333,10 +341,14 @@
     store(head_done, head_out, LANGS)
     loads[1].wait()
     store(loss_got, loss_out, LANGS + 1)
-    for e, skip in enumerate(skips):
-        loads[2 + e].wait()
+    for n, (e, h) in enumerate(pieces):
+        loads[2 + n].wait()
+        skip = skips[e]
+        here = pl.ds(h * piece, piece)
         store(
-            back_got.at[e, :, pl.ds(skip, wide - skip)], state_out.at[:, pl.ds(e * wide, wide - skip)], e
+            back_got.at[e, here, pl.ds(skip, wide - skip)],
+            state_out.at[here, pl.ds(e * wide, wide - skip)],
+            LANGS + 2 + n,
         )
     for copy in stores:
         copy.wait()
@@ -350,7 +362,6 @@
     half = BLOCK // 2
     group = LANGS * rows
     hbm = pl.BlockSpec(memory_space=pl.ANY)
-    vmem = pl.BlockSpec(memory_space=pltpu.VMEM)
     dma = pltpu.SemaphoreType.DMA
     three, batches = dma((3,)), dma((3 * BATCHES,))
     loss, back, head = pl.pallas_call(
@@ -361,12 +372,13 @@
             jax.ShapeDtypeStruct((LANGS, share, wide), BF16),
         ),
         in_specs=[hbm] * 6,
-        out_specs=(vmem, hbm, hbm),
+        out_specs=[hbm] * 3,
         scratch_shapes=[
             pltpu.SMEM((LANGS,), jnp.int32),
             pltpu.VMEM((LANGS, 1, rows), jnp.int32),
             pltpu.VMEM((1, rows), jnp.int32),
             pltpu.VMEM((1, rows), BF16),
+            pltpu.VMEM((1, rows), F32),
             pltpu.VMEM((group, wide), BF16),
             pltpu.VMEM((LANGS * BLOCK, wide), BF16),
             pltpu.VMEM((group, BLOCK), F32),
@@ -381,7 +393,7 @@
             pltpu.VMEM((LANGS - 1, half, wide), BF16),
             pltpu.VMEM((LANGS - 1, half, wide), BF16),
             pltpu.VMEM((LANGS, share, wide), BF16),
-            dma((4,)), dma((2 * BATCHES + 2,)), three, three, three, three, three, three, batches, batches,
+            dma((4,)), dma((2 * BATCHES + 3,)), three, three, three, three, three, three, batches, batches,
             batches, batches, batches, batches, batches, batches, dma((LANGS,)), dma((LANGS,)),
             three, three, three, three,
         ],
@@ -411,8 +423,8 @@
             pltpu.VMEM((LANGS, rows, wide), BF16),
             pltpu.VMEM((LANGS, share, wide), BF16),
             pltpu.VMEM((1, share, width), F32),
-            dma((LANGS + 2,)),
-            dma((LANGS + 2,)),
+            dma((3 * LANGS + 2,)),
+            dma((3 * LANGS + 2,)),
         ],
         compiler_params=pltpu.CompilerParams(vmem_limit_bytes=60 * 1024 * 1024),
         name="joined",

time: 57 us -> 56.6 us (level)
    pallas_call x1, Pallas kernels: 53.4 us -> 52.8 us  [sliced(): pl.pallas_call(sliced_kernel, out_shape=(jax.ShapeDtypeStruct((1, rows),...]
where the time goes in v10:
time: 56.6 us; the launch traced here: 55.8 us
  Pallas kernels  55.2 us (98%)
  between operations  0.64 us (1%)
    pallas_call x1, Pallas kernels, sliced(): pl.pallas_call(sliced_kernel, out_shape=(jax.ShapeDtypeStruct((1, rows),...  52.8 us
    pallas_call x1, Pallas kernels, sliced(): pl.pallas_call(joined_kernel, out_shape=(jax.ShapeDtypeStruct((1, rows),...  2.39 us

profile of v10, /device:TPU:0, one launch (start us, length us, event | category | flops | bytes accessed | tf_op | source)
XLA Modules:
  0.0 55.8 jit_solution(6815844781094557907)
XLA Ops:
  0.6 52.8 %sliced.1 = (f32[1,128]{1,0:T(1,128)}, bf16[4,128,1408]{2,1,0:T(8,128)(2,1)}, bf16[4,16,1408]{2,1,0:T(8,128)(2,1)}) custom-call(s32[4]{0:T(128)} %order_in.1, s32[1,128]{1,0:T(1,128)} %bitcast.6, s32[1,128]{1,0:T(1,128)} %bitcast.7, bf16[1,128]{1,0:T(2,128)(2,1)} %bitcast.8, bf16[128,5376]{1,0:T(8,128)(2,1)} %states.1, bf16[128,5376]{1,0:T(8,128)(2,1)} %bitcast.5), custom_call_target="tpu_custom_call" | custom-call | tf_op jit(solution)/shard_map/sliced/pallas_call | solution.py:367
  53.4 2.4 %joined.1 = (f32[1,128]{1,0:T(1,128)}, bf16[128,5376]{1,0:T(8,128)(2,1)}, f32[1,16,5376]{2,1,0:T(8,128)}) custom-call(f32[1,128]{1,0:T(1,128)} %get-tuple-element.9.loss_in, bf16[4,128,1408]{2,1,0:T(8,128)(2,1)} %get-tuple-element.10.back_in, bf16[4,16,1408]{2,1,0:T(8,128)(2,1)} %get-tuple-element.11.head_in), custom_call_target="tpu_custom_call" | custom-call | tf_op jit(solution)/shard_map/joined/pallas_call | solution.py:412
